TPU v7x, 128 devices: a whole 4x4x4 slice. The times are simulated.
128 devices in a mesh: fsdp: 16 (over x_lo, y, core), sp: 8 (over x_hi, z).
Axes of the slice: x: 4 (x_hi: 2, x_lo: 2; x = x_hi * 2 + x_lo), y: 4, z: 4, core: 2. Of those that a mesh axis runs over, the one named last changes fastest.
Arguments:
- tokens: bfloat16 [16, 1024, 1024], P('fsdp', 'sp'), may hold values from -6 to 6
- cotangent: bfloat16 [16, 1024, 1024], P('fsdp', 'sp'), may hold values from -6 to 6
- w_qkv: bfloat16 [1024, 3072], P('fsdp'), may hold values from -0.1875 to 0.1875
- bias_q: bfloat16 [1024], P('fsdp'), may hold values from -3 to 3
- bias_v: bfloat16 [1024], P('fsdp'), may hold values from -0.125 to 0.125
- w_out: bfloat16 [1024, 1024], P('fsdp'), may hold values from -3 to 3
- bias_out: bfloat16 [1024], P('fsdp'), may hold values from -3 to 3
- gain_one: bfloat16 [1024], P('fsdp'), may hold values from 0.5 to 1.5
- shift_one: bfloat16 [1024], P('fsdp'), may hold values from -3 to 3
- w_up: bfloat16 [1024, 4096], P('fsdp'), may hold values from -0.1875 to 0.1875
- bias_up: bfloat16 [4096], P('fsdp'), may hold values from -3 to 3
- w_down: bfloat16 [4096, 1024], P('fsdp'), may hold values from -0.09375 to 0.09375
- bias_down: bfloat16 [1024], P('fsdp'), may hold values from -3 to 3
- gain_two: bfloat16 [1024], P('fsdp'), may hold values from 0.5 to 1.5
- shift_two: bfloat16 [1024], P('fsdp'), may hold values from -3 to 3
Outputs:
- output: bfloat16 [16, 1024, 1024], P('fsdp', 'sp')
- grad_tokens: bfloat16 [16, 1024, 1024], P('fsdp', 'sp')
- grad_w_qkv: float32 [1024, 3072], P('fsdp')
- grad_bias_q: float32 [1024], P('fsdp')
- grad_bias_v: float32 [1024], P('fsdp')
- grad_w_out: float32 [1024, 1024], P('fsdp')
- grad_bias_out: float32 [1024], P('fsdp')
- grad_gain_one: float32 [1024], P('fsdp')
- grad_shift_one: float32 [1024], P('fsdp')
- grad_w_up: float32 [1024, 4096], P('fsdp')
- grad_bias_up: float32 [4096], P('fsdp')
- grad_w_down: float32 [4096, 1024], P('fsdp')
- grad_bias_down: float32 [1024], P('fsdp')
- grad_gain_two: float32 [1024], P('fsdp')
- grad_shift_two: float32 [1024], P('fsdp')
All inputs are finite; a program needn't handle non-finite values.
Results may differ from a plain program's by a relative error of at most 0.024.
Values may be sent and summed in bfloat16 or wider, within the bound.
A program may use at most 128 MiB of HBM per device.

v0:
```python
import functools
import math

import jax
import jax.numpy as jnp
from jax import lax
from jax.experimental import pallas as pl
from jax.experimental.pallas import tpu as pltpu
from jax.sharding import PartitionSpec as P

HD = 64
MESH = pl.DeviceIdType.MESH
BF = jnp.bfloat16
F32 = jnp.float32

epsilon = 1e-05
root_half = 0.7071067811865476
inv_root_two_pi = 0.3989422804014327


class Place:
    def __init__(self):
        f = lax.axis_index("fsdp")
        s = lax.axis_index("sp")
        self.xh, self.xl, self.y, self.z, self.c = s // 4, f // 8, (f // 2) % 4, s % 4, f % 2
        self.x = 2 * self.xh + self.xl

    def to(self, dx=0, dy=0, dz=0, dc=0):
        x = lax.rem(self.x + dx + 4, 4)
        y = lax.rem(self.y + dy + 4, 4)
        z = lax.rem(self.z + dz + 4, 4)
        c = self.c if dc == 0 else 1 - self.c
        return ((x % 2) * 8 + y * 2 + c, (x // 2) * 4 + z)


class Copies:
    def __init__(self, send, recv):
        self.send, self.recv, self.n = send, recv, 0

    def remote(self, src, dst, dev):
        i = self.n
        self.n += 1
        cp = pltpu.make_async_remote_copy(
            src_ref=src,
            dst_ref=dst,
            send_sem=self.send.at[i],
            recv_sem=self.recv.at[i],
            device_id=dev,
            device_id_type=MESH,
        )
        cp.start()
        return cp

    def local(self, src, dst):
        i = self.n
        self.n += 1
        cp = pltpu.make_async_copy(src, dst, self.recv.at[i])
        cp.start()
        return cp


def greet(targets):
    bar = pltpu.get_barrier_semaphore()
    for t in targets:
        pl.semaphore_signal(bar, inc=1, device_id=t, device_id_type=MESH)
    pl.semaphore_wait(bar, len(targets))


class Gather:
    def __init__(self, place, copies, src, out, lo, n, quarters):
        self.p, self.s, self.src, self.out = place, copies, src, out
        self.lo, self.n, self.quarters = lo, n, quarters
        self.sent, self.core = [], []

    def cols(self, half=None):
        if half is None:
            return pl.ds(self.lo, self.n)
        return pl.ds(self.lo + half * (self.n // 2), self.n // 2)

    def go(self, src, dst, **k):
        cp = self.s.remote(src, dst, self.p.to(**k))
        self.sent.append(cp)
        return cp

    def q(self):
        return self.p.z if self.quarters else slice(None)

    def start(self):
        p, o, q = self.p, self.out, self.q()
        self.own = self.s.local(
            self.src.at[:, :, self.cols()], o.at[p.xl, p.y, p.c, :, :, self.cols()]
        )
        self.ycp = [
            self.go(
                self.src.at[q, :, self.cols()], o.at[p.xl, p.y, p.c, q, :, self.cols()], dy=k
            )
            for k in (1, 3, 2)
        ]
        self.xcp = [
            self.go(
                self.src.at[q, :, self.cols(h)], o.at[p.xl, p.y, p.c, q, :, self.cols(h)], dx=dx
            )
            for h, dx in ((0, 1), (1, -1))
        ]

    def stage_x(self):
        p, o, q = self.p, self.out, self.q()
        for k, cp in zip((3, 1, 2), self.ycp):
            cp.wait_recv()
            for h, dx in ((0, 1), (1, -1)):
                r = o.at[p.xl, lax.rem(p.y + k, 4), p.c, q, :, self.cols(h)]
                self.xcp.append(self.go(r, r, dx=dx))
        if self.quarters:
            self.zcp = []
            for dz in (1, 3, 2):
                for k in (1, 2, 3):
                    r = o.at[p.xl, lax.rem(p.y + k, 4), p.c, q, :, self.cols()]
                    self.zcp.append(self.go(r, r, dz=dz))
        else:
            self.own.wait()
            r = o.at[p.xl, :, p.c, :, :, self.cols()]
            self.core.append(self.go(r, r, dc=1))

    def stage_z(self):
        if not self.quarters:
            return
        p, o, q = self.p, self.out, self.q()
        for cp in self.xcp:
            cp.wait_recv()
        for dz in (1, 3, 2):
            r = o.at[1 - p.xl, :, p.c, q, :, self.cols()]
            self.zcp.append(self.go(r, r, dz=dz))

    def stage_core(self):
        p, o = self.p, self.out
        if self.quarters:
            for cp in self.zcp:
                cp.wait_recv()
            self.own.wait()
            r = o.at[p.xl, :, p.c, :, :, self.cols()]
            self.core.append(self.go(r, r, dc=1))
        else:
            for cp in self.xcp:
                cp.wait_recv()
        r = o.at[1 - p.xl, :, p.c, :, :, self.cols()]
        self.core.append(self.go(r, r, dc=1))

    def arrived(self):
        for cp in self.core:
            cp.wait_recv()
        self.core = []

    def finish(self):
        self.arrived()
        for cp in self.sent:
            cp.wait_send()


class Reduce:
    def __init__(self, place, copies, order, g, bufs, total):
        self.p, self.s, self.order, self.g = place, copies, order, g
        self.r1, self.s1, self.r2, self.s2, self.r3 = bufs
        self.tot = total
        self.n = g.shape[-1]
        self.sent = []

    def go(self, src, dst, **k):
        cp = self.s.remote(src, dst, self.p.to(**k))
        self.sent.append(cp)
        return cp

    def half(self, xh):
        m = self.n // 2
        return pl.ds(pl.multiple_of(xh * m, 128), m)

    def me(self, i):
        return {"x": self.p.x, "y": self.p.y, "z": self.p.z}[self.order[i]]

    def pick(self, ref, i, v):
        o, ax = self.order, self.order[i]
        if ax == "x":
            rest = [slice(None)] * (len(ref.shape) - 2)
            return ref.at[(lax.rem(v, 2),) + tuple(rest) + (self.half(v // 2),)]
        lead = 0 if "x" in o[:i] else 1
        if ax == "z" and "y" not in o[:i]:
            lead += 1
        return ref.at[(slice(None),) * lead + (v,)]

    def scatter(self, i, src, recv):
        me = self.me(i)
        return [
            self.go(
                self.pick(src, i, lax.rem(me + k, 4)), recv.at[k - 1], **{"d" + self.order[i]: k}
            )
            for k in (1, 3, 2)
        ]

    def add(self, i, src, recv, out, cps):
        for cp in cps:
            cp.wait_recv()
        own = self.pick(src, i, self.me(i))
        shape = out.shape
        rows = (slice(None), slice(None))

        def one(idx):
            acc = own[idx].astype(F32)
            for k in range(3):
                acc = acc + recv[(k,) + idx].astype(F32)
            out[idx] = acc.astype(out.dtype)

        if len(shape) == 2:
            one(rows)
            return

        def body(j, _):
            idx = []
            for d in reversed(shape[:-2]):
                idx.insert(0, lax.rem(j, d))
                j = j // d
            one(tuple(idx) + rows)
            return 0

        lax.fori_loop(0, math.prod(shape[:-2]), body, 0)

    def first(self):
        self.c1 = self.scatter(0, self.g, self.r1)

    def second(self):
        self.add(0, self.g, self.r1, self.s1, self.c1)
        self.c2 = self.scatter(1, self.s1, self.r2)

    def third(self):
        self.add(1, self.s1, self.r2, self.s2, self.c2)
        self.c3 = self.scatter(2, self.s2, self.r3)

    def share(self):
        p = self.p
        mine = self.tot.at[p.z, :, self.half(p.xh)]
        self.add(2, self.s2, self.r3, mine, self.c3)
        self.c4 = self.go(mine, mine, dx=2)

    def spread(self):
        self.c4.wait_recv()
        r = self.tot.at[self.p.z]
        self.c5 = [self.go(r, r, dz=k) for k in (1, 3, 2)]

    def done(self):
        for cp in self.c5:
            cp.wait_recv()

    def finish(self):
        for cp in self.sent:
            cp.wait_send()


def reduce_shapes(order, q, n):
    full = {"x": 2, "y": 4, "z": 4}
    left, width, out = ["x", "y", "z"], n, []
    for i, ax in enumerate(order):
        left.remove(ax)
        if ax == "x":
            width = n // 2
        s = tuple(full[a] for a in left) + (q, width)
        out.append((3,) + s)
        if i < 2:
            out.append(s)
    return out


def run_pipe(steps, offsets, count):
    for t in range(count + max(offsets)):
        for step, d in zip(steps, offsets):
            if 0 <= t - d < count:
                step(t - d)


ROWS = {"small": 16, "out": 64, "up": 64, "down": 256}
COLS = {"small": 256, "out": 1024, "up": 4096, "down": 1024}
GATHER_NAMES = ("small", "out", "up", "down")
GATHER_PARTS = (
    ("small", 0, 256, False),
    ("out", 0, 1024, False),
    ("up", 0, 1024, True),
    ("up", 1024, 1024, False),
    ("up", 2048, 1024, True),
    ("up", 3072, 1024, False),
    ("down", 0, 512, False),
    ("down", 512, 512, False),
)
ANYWHERE = pl.BlockSpec(memory_space=pl.ANY)
INSIDE = pl.BlockSpec(memory_space=pltpu.VMEM)


def flat_pipe(steps, offsets, count):
    out = []
    for t in range(count + max(offsets)):
        for step, d in zip(steps, offsets):
            if 0 <= t - d < count:
                out.append(functools.partial(step, t - d))
    return out


def advance(queue, n):
    for _ in range(min(n, len(queue))):
        queue.pop(0)()


def sp_peers(p):
    out = []
    for dx, dz in ((0, 1), (0, 3), (2, 0), (2, 1), (2, 3), (0, 2), (2, 2)):
        xh = p.xh if dx == 0 else 1 - p.xh
        out.append((p.to(dx=dx, dz=dz), xh * 4 + lax.rem(p.z + dz, 4)))
    return out


def nt(a, b):
    return lax.dot_general(a, b, (((1,), (1,)), ((), ())), preferred_element_type=F32)


def nn(a, b):
    return jnp.dot(a, b, preferred_element_type=F32)


def forward_kernel(*refs):
    refs = list(refs)

    def take(n):
        head = refs[:n]
        del refs[:n]
        return head

    k = len(GATHER_NAMES)
    tok, wq = take(2)
    vectors, bias_up = take(2)
    ins = dict(zip(GATHER_NAMES[1:], take(k - 1)))
    outs = dict(zip(GATHER_NAMES, take(k)))
    tall, wsel, qkv, lse, ctx = take(5)
    small_v, pack, vt, ct, ch, cr = take(6)
    p, s = Place(), Copies(*refs)
    me = p.xh * 4 + p.z
    peers = sp_peers(p)
    pack[...] = jnp.zeros_like(pack)
    pack[0, 0:8, 0:64] = vectors[...]
    pack[0, 0:8, 192:256] = vectors[...]
    pack[0, 8:9, :] = bias_up[...]
    ins["small"] = pack
    greet(
        [p.to(dy=1), p.to(dy=2), p.to(dy=3), p.to(dx=1), p.to(dx=3), p.to(dc=1)]
        + [d for d, _ in peers]
    )
    sent = []

    def go(src, dst, dev):
        cp = s.remote(src, dst, dev)
        sent.append(cp)
        return cp

    pick = [
        s.local(
            wq.at[:, pl.ds(pl.multiple_of(j * 1024 + me * 128, 128), 128)],
            wsel.at[p.xl, p.y, p.c, :, pl.ds(j * 128, 128)],
        )
        for j in range(3)
    ]
    own_tok = s.local(tok, tall.at[me])
    tok_cps = [go(tok, tall.at[me], d) for d, _ in peers]
    parts = [Gather(p, s, ins[m], outs[m], lo, n, quarters) for m, lo, n, quarters in GATHER_PARTS]
    parts[0].start()
    for cp in pick:
        cp.wait()
    mine = wsel.at[p.xl, p.y, p.c]
    wy = [go(mine, mine, p.to(dy=d)) for d in (1, 3, 2)]
    queue = flat_pipe(
        (
            lambda i: parts[i + 1].start(),
            lambda i: parts[i + 1].stage_x(),
            lambda i: parts[i + 1].stage_z(),
            lambda i: parts[i + 1].stage_core(),
        ),
        (0, 3, 5, 6),
        len(parts) - 1,
    )
    advance(queue, 2)
    for cp in wy:
        cp.wait_recv()
    column = wsel.at[p.xl, :, p.c]
    wx = go(column, column, p.to(dx=1 - 2 * p.xl))
    parts[0].stage_x()
    advance(queue, 1)
    wx.wait_recv()
    plane = wsel.at[:, :, p.c]
    wc = go(plane, plane, p.to(dc=1))
    parts[0].stage_core()
    advance(queue, 1)
    parts[0].arrived()
    small_cp = s.local(outs["small"], small_v)
    advance(queue, 2)
    wc.wait_recv()
    small_cp.wait()
    own_tok.wait()
    for cp in tok_cps:
        cp.wait_recv()

    b, y = me // 4, me % 4
    qv = [
        small_v[b, y, 0, 0, r : r + 1, 0:128] + small_v[b, y, 1, 0, r : r + 1, 128:256]
        for r in range(2)
    ]
    bias = jnp.concatenate([qv[0], jnp.zeros((1, 128), F32), qv[1]], axis=1)

    def project(i, _):
        x = tall[pl.ds(2 * i, 2)].reshape(256, 1024)
        v = nn(x, wsel[...].reshape(1024, 384)) + bias
        qkv[pl.ds(pl.multiple_of(i * 256, 256), 256), :] = v.astype(BF)
        return 0

    lax.fori_loop(0, 4, project, 0)
    vt[...] = qkv[:, 256:384].astype(F32).T.astype(BF)
    per = max(1, (len(queue) - 4) // 4)
    for b in range(4):
        rows = pl.ds(b * 256, 256)
        for h in range(2):
            keys = qkv[:, 128 + 64 * h : 192 + 64 * h]
            st = nt(keys, qkv[rows, 64 * h : 64 * h + 64]) * 0.125
            peak = jnp.max(st, axis=0, keepdims=True)
            e = jnp.exp(st - peak)
            total = jnp.sum(e, axis=0, keepdims=True)
            c = nn(vt[64 * h : 64 * h + 64, :], e.astype(BF))
            ct[64 * h : 64 * h + 64, rows] = c / total
            lse[h : h + 1, rows] = peak + jnp.log(total)
        advance(queue, per)
    for t in range(8):
        ch[t] = ct[:, t * 128 : (t + 1) * 128].T.astype(BF)
    ctx_cps = [go(ch.at[t], cr.at[me], d) for d, t in peers]
    cr[me] = ch[me]
    advance(queue, len(queue))
    for cp in ctx_cps:
        cp.wait_recv()
    for t in range(8):
        ctx[:, t * 128 : (t + 1) * 128] = cr[t]
    for g in parts:
        g.finish()
    for cp in sent:
        cp.wait_send()


def attend_forward(tokens, w_qkv, vectors, bias_up, arrays):
    ins = []
    shapes = [jax.ShapeDtypeStruct((2, 4, 2, 1, 16, 256), F32)]
    for m, a in zip(GATHER_NAMES[1:], arrays):
        ins.append(a.reshape(4, ROWS[m] // 4, COLS[m]))
        shapes.append(jax.ShapeDtypeStruct((2, 4, 2) + ins[-1].shape, BF))
    k = len(shapes)
    shapes += [
        jax.ShapeDtypeStruct((8, 128, 1024), BF),
        jax.ShapeDtypeStruct((2, 4, 2, 64, 384), BF),
        jax.ShapeDtypeStruct((1024, 384), BF),
        jax.ShapeDtypeStruct((8, 1024), F32),
        jax.ShapeDtypeStruct((128, 1024), BF),
    ]
    out = pl.pallas_call(
        forward_kernel,
        out_shape=shapes,
        in_specs=[ANYWHERE] * 2 + [INSIDE] * 2 + [ANYWHERE] * (k - 1),
        out_specs=[ANYWHERE] * k + [INSIDE] * 5,
        scratch_shapes=[
            pltpu.VMEM((2, 4, 2, 1, 16, 256), F32),
            pltpu.VMEM((1, 16, 256), F32),
            pltpu.VMEM((128, 1024), BF),
            pltpu.VMEM((128, 1024), F32),
            pltpu.VMEM((8, 128, 128), BF),
            pltpu.VMEM((8, 128, 128), BF),
            pltpu.SemaphoreType.DMA((200,)),
            pltpu.SemaphoreType.DMA((200,)),
        ],
        compiler_params=pltpu.CompilerParams(
            collective_id=1, has_side_effects=True, vmem_limit_bytes=40 * 2**20
        ),
        name="attend_forward",
    )(tokens, w_qkv, vectors, bias_up, *ins)
    whole = [o.reshape(16 * ROWS[m], COLS[m]) for m, o in zip(GATHER_NAMES[1:], out[1:k])]
    return [out[0]] + whole + list(out[k:])


SMALL_SHAPE = (2, 4, 4, 8, 256)


class Products:
    def __init__(self, place, copies, left, right, both_left, both_right, totals, pieces, g, bufs):
        self.p, self.s = place, copies
        self.left, self.right = left, right
        self.both_left, self.both_right = both_left, both_right
        self.pieces, self.g = pieces, g
        self.swaps, self.ready = {}, set()
        self.red = [
            Reduce(place, copies, o, gi, b, totals[m].at[:, :, pl.ds(lo, n)])
            for (m, lo, n, o), gi, b in zip(pieces, g, bufs)
        ]

    def swap(self, m):
        p, s = self.p, self.s
        here = [
            s.local(self.left[m].at[:, :, p.c], self.both_left[m].at[:, :, :, pl.ds(0, 128)]),
            s.local(self.right[m], self.both_right[m].at[pl.ds(0, 128)]),
        ]
        there = [
            s.remote(
                self.left[m].at[:, :, 1 - p.c],
                self.both_left[m].at[:, :, :, pl.ds(128, 128)],
                p.to(dc=1),
            ),
            s.remote(self.right[m], self.both_right[m].at[pl.ds(128, 128)], p.to(dc=1)),
        ]
        self.swaps[m] = (here, there)

    def begin(self, i):
        m, lo, n, _ = self.pieces[i]
        if m not in self.ready:
            for cp in self.swaps[m][0]:
                cp.wait()
            for cp in self.swaps[m][1]:
                cp.wait_recv()
            self.ready.add(m)
        left, right, g = self.both_left[m], self.both_right[m], self.g[i]
        rows = left.shape[2]
        tile = min(512, n)

        def body(j, _):
            b, t = j // (n // tile), lax.rem(j, n // tile)
            c0 = pl.multiple_of(lo + t * tile, tile)
            v = jnp.dot(
                left[b].reshape(4 * rows, 256),
                right[:, pl.ds(c0, tile)],
                preferred_element_type=F32,
            ).astype(BF)
            g[b, :, :, :, pl.ds(pl.multiple_of(t * tile, tile), tile)] = v.reshape(
                4, 4, rows // 4, tile
            )
            return 0

        lax.fori_loop(0, 2 * (n // tile), body, 0)
        self.red[i].first()

    def finish(self):
        for r in self.red:
            r.finish()
        for m in self.swaps:
            for cp in self.swaps[m][1]:
                cp.wait_send()


def piece_scratch(pieces):
    sc = []
    for m, _, n, o in pieces:
        q = ROWS[m] // 4
        sc.append(pltpu.VMEM((2, 4, 4, q, n), BF))
        sc += [pltpu.VMEM(x, BF) for x in reduce_shapes(o, q, n)]
    return sc


VECTORS = (
    "bias_q",
    "bias_v",
    "bias_out",
    "gain_one",
    "shift_one",
    "bias_down",
    "gain_two",
    "shift_two",
)


def ln_rows(u):
    center = u - jnp.mean(u, axis=-1, keepdims=True)
    spread = jnp.mean(center * center, axis=-1, keepdims=True)
    inverse = lax.rsqrt(spread + epsilon)
    return center * inverse, inverse


def ln_back(e, hat, inverse, gain):
    scaled = e * gain
    centered = scaled - jnp.mean(scaled, axis=-1, keepdims=True)
    return inverse * (centered - hat * jnp.mean(scaled * hat, axis=-1, keepdims=True))


def col_sum(v):
    return jnp.sum(v, axis=0, keepdims=True)


def middle(
    tok,
    ctx,
    cot,
    small_v,
    wait_out,
    wait_up,
    wait_down,
    w_out,
    w_up,
    w_down,
    output,
    gctx,
    gsum,
    lefts,
    rights,
    small,
    vec,
    bup,
    slope,
    hat1,
    base,
    acc,
):
    for r, name in enumerate(VECTORS):
        for j in range(8):
            a = small_v[j // 4, j % 4, 0, 0, r : r + 1, 0:128]
            b = small_v[j // 4, j % 4, 1, 0, r : r + 1, 128:256]
            vec[r : r + 1, j * 128 : (j + 1) * 128] = a + b
    for f in range(16):
        bup[0:1, f * 256 : (f + 1) * 256] = small_v[f // 8, (f // 2) % 4, f % 2, 0, 8:9, :]
    row = {n: vec[r : r + 1, :] for r, n in enumerate(VECTORS)}

    def put(name, v):
        r = VECTORS.index(name)
        for j in range(8):
            small[j // 4, j % 4, 0, r : r + 1, 0:128] = v[:, j * 128 : (j + 1) * 128]

    small[...] = jnp.zeros_like(small)
    x = tok[...].astype(F32)
    wait_out()
    branch = nn(ctx[...], w_out[...]) + row["bias_out"]
    hat, inv1 = ln_rows(x + branch)
    hat1[...] = hat
    normed = hat * row["gain_one"] + row["shift_one"]
    base[...] = normed
    low = normed.astype(BF)
    rights["low"][...] = low
    lefts["up"][...] = normed.T.astype(BF).reshape(8, 2, 64, 128)
    lefts["out"][...] = ctx[...].astype(F32).T.astype(BF).reshape(8, 2, 64, 128)
    acc[...] = jnp.zeros_like(acc)

    def up(t, _):
        cols = pl.ds(pl.multiple_of(t * 512, 512), 512)
        wait_up(t)
        pre = nn(rights["low"][...], w_up[t]) + bup[0:1, cols]
        cdf = 0.5 * (1.0 + lax.erf(pre * root_half))
        slope[:, cols] = cdf + pre * jnp.exp(-0.5 * pre * pre) * inv_root_two_pi
        act = pre * cdf
        lefts["down"][t] = act.T.astype(BF).reshape(2, 256, 128)
        wait_down(t)
        acc[...] += nn(act.astype(BF), w_down[t])
        return 0

    lax.fori_loop(0, 8, up, 0)
    hat2, inv2 = ln_rows(base[...] + acc[...] + row["bias_down"])
    output[...] = (hat2 * row["gain_two"] + row["shift_two"]).astype(BF)
    dy = cot[...].astype(F32)
    put("gain_two", col_sum(dy * hat2))
    put("shift_two", col_sum(dy))
    gs2 = ln_back(dy, hat2, inv2, row["gain_two"])
    acc[...] = gs2
    ffn = gs2.astype(BF)
    rights["down"][...] = ffn
    put("bias_down", col_sum(ffn.astype(F32)))

    def back(t, _):
        cols = pl.ds(pl.multiple_of(t * 512, 512), 512)
        pre = (nt(rights["down"][...], w_down[t]) * slope[:, cols]).astype(BF)
        rights["up"][:, cols] = pre
        s = col_sum(pre.astype(F32))
        small[t // 4, lax.rem(t, 4), 1, 0:1, :] = s[:, :256]
        small[t // 4, lax.rem(t, 4), 1, 1:2, :] = s[:, 256:]
        acc[...] += nt(pre, w_up[t])
        return 0

    lax.fori_loop(0, 8, back, 0)
    gn = acc[...]
    hat = hat1[...]
    put("gain_one", col_sum(gn * hat))
    put("shift_one", col_sum(gn))
    gs1 = ln_back(gn, hat, inv1, row["gain_one"])
    gsum[...] = gs1
    gb = gs1.astype(BF)
    rights["out"][...] = gb
    put("bias_out", col_sum(gb.astype(F32)))
    gctx[...] = nt(gb, w_out[...]).astype(BF)


def middle_kernel(
    tok, ctx, cot, small_h, out_h, up_h, down_h,
    output, gctx, gsum, l_down, l_up, l_out, r_down, r_up, r_out, small,
    small_v, w_out, w_up, w_down, low, vec, bup, slope, hat1, base, acc, sem,
):
    cps = [pltpu.make_async_copy(small_h, small_v, sem.at[0])]
    cps += [pltpu.make_async_copy(out_h, w_out, sem.at[1])]
    ups = [
        pltpu.make_async_copy(up_h.at[:, pl.ds(t * 512, 512)], w_up.at[t], sem.at[2 + t])
        for t in range(8)
    ]
    downs = [
        pltpu.make_async_copy(down_h.at[pl.ds(t * 512, 512)], w_down.at[t], sem.at[10 + t])
        for t in range(8)
    ]
    for cp in cps:
        cp.start()
    for a, b in zip(ups, downs):
        a.start()
        b.start()
    cps[0].wait()

    def wait_up(t):
        pltpu.make_async_copy(up_h.at[:, pl.ds(0, 512)], w_up.at[t], sem.at[2 + t]).wait()

    def wait_down(t):
        pltpu.make_async_copy(down_h.at[pl.ds(0, 512)], w_down.at[t], sem.at[10 + t]).wait()

    middle(
        tok, ctx, cot, small_v, cps[1].wait, wait_up, wait_down, w_out, w_up, w_down,
        output, gctx, gsum,
        {"down": l_down, "up": l_up, "out": l_out},
        {"down": r_down, "up": r_up, "out": r_out, "low": low},
        small, vec, bup, slope, hat1, base, acc,
    )


def run_middle(tok, ctx, cot, small_full, full_out, full_up, full_down):
    def b(*s):
        return jax.ShapeDtypeStruct(s, BF)

    def f(*s):
        return jax.ShapeDtypeStruct(s, F32)

    return pl.pallas_call(
        middle_kernel,
        out_shape=[b(128, 1024), b(128, 1024), f(128, 1024)]
        + [b(8, 2, 256, 128), b(8, 2, 64, 128), b(8, 2, 64, 128)]
        + [b(128, 1024), b(128, 4096), b(128, 1024), f(2, 4, 4, 8, 256)],
        in_specs=[INSIDE] * 3 + [ANYWHERE] * 4,
        out_specs=[INSIDE] * 10,
        scratch_shapes=[
            pltpu.VMEM((2, 4, 2, 1, 16, 256), F32),
            pltpu.VMEM((1024, 1024), BF),
            pltpu.VMEM((8, 1024, 512), BF),
            pltpu.VMEM((8, 512, 1024), BF),
            pltpu.VMEM((128, 1024), BF),
            pltpu.VMEM((8, 1024), F32),
            pltpu.VMEM((8, 4096), F32),
            pltpu.VMEM((128, 4096), F32),
            pltpu.VMEM((128, 1024), F32),
            pltpu.VMEM((128, 1024), F32),
            pltpu.VMEM((128, 1024), F32),
            pltpu.SemaphoreType.DMA((18,)),
        ],
        compiler_params=pltpu.CompilerParams(vmem_limit_bytes=56 * 2**20),
        name="middle",
    )(tok, ctx, cot, small_full, full_out, full_up, full_down)


PIECES = (
    ("down", 0, 512, "yzx"),
    ("up", 0, 1024, "xyz"),
    ("down", 512, 512, "zxy"),
    ("up", 1024, 1024, "yzx"),
    ("up", 2048, 1024, "zxy"),
    ("up", 3072, 1024, "xyz"),
    ("out", 0, 1024, "yzx"),
)
GRAD_NAMES = ("down", "up", "out")


def backward_kernel(*refs):
    refs = list(refs)

    def take(n):
        head = refs[:n]
        del refs[:n]
        return head

    k = len(GRAD_NAMES)
    left = dict(zip(GRAD_NAMES, take(k)))
    right = dict(zip(GRAD_NAMES, take(k)))
    small, gctx, gsum, tall_t, wsel, qkv, lse = take(7)
    totals = dict(zip(GRAD_NAMES, take(k)))
    small_total, grad_tok, gw = take(3)
    both_left = dict(zip(GRAD_NAMES, take(k)))
    both_right = dict(zip(GRAD_NAMES, take(k)))
    small_src, small_in, small_g = take(3)
    small_bufs = take(5)
    g, bufs = [], []
    for _ in PIECES:
        g += take(1)
        bufs.append(take(5))
    do, kt, dqt, dkv, dqkv, gq, gq_c, gq_x, gq_y, dts, dtr = take(11)
    p, s = Place(), Copies(*refs)
    me = p.xh * 4 + p.z
    peers = sp_peers(p)
    greet(
        [p.to(dy=1), p.to(dy=2), p.to(dy=3), p.to(dx=1), p.to(dx=3), p.to(dc=1)]
        + [d for d, _ in peers]
    )
    sent = []

    def go(src, dst, dev):
        cp = s.remote(src, dst, dev)
        sent.append(cp)
        return cp

    do_cps = [
        go(gctx.at[:, pl.ds(pl.multiple_of(t * 128, 128), 128)], do.at[me], d) for d, t in peers
    ]
    do_own = s.local(gctx.at[:, pl.ds(pl.multiple_of(me * 128, 128), 128)], do.at[me])
    prod = Products(p, s, left, right, both_left, both_right, totals, PIECES, g, bufs)
    for m in GRAD_NAMES:
        prod.swap(m)
    kt[...] = qkv[:, 128:256].astype(F32).T.astype(BF)
    red = prod.red
    n = len(PIECES)
    for i in range(n):
        prod.begin(i)
    queue = flat_pipe(
        (
            lambda i: red[i].second(),
            lambda i: red[i].third(),
            lambda i: red[i].share(),
            lambda i: red[i].spread(),
            lambda i: red[i].done(),
        ),
        (0, 2, 4, 5, 6),
        n,
    )
    do_own.wait()
    for cp in do_cps:
        cp.wait_recv()
    dkv[...] = jnp.zeros_like(dkv)
    for b in range(4):
        rows = pl.ds(b * 256, 256)
        for h in range(2):
            lanes = slice(64 * h, 64 * h + 64)
            keys = qkv[:, 128 + 64 * h : 192 + 64 * h]
            vals = qkv[:, 256 + 64 * h : 320 + 64 * h]
            q = qkv[rows, lanes]
            dob = do[2 * b : 2 * b + 2].reshape(256, 128)[:, lanes]
            probs = jnp.exp(nt(keys, q) * 0.125 - lse[h : h + 1, rows])
            dp = nt(vals, dob)
            inner = jnp.sum(probs * dp, axis=0, keepdims=True)
            ds = (probs * (dp - inner)).astype(BF)
            dqt[lanes, rows] = nn(kt[lanes, :], ds) * 0.125
            dkv[:, lanes] += nn(ds, q) * 0.125
            dkv[:, 128 + 64 * h : 192 + 64 * h] += nn(probs.astype(BF), dob)
        if b >= 1:
            advance(queue, 1)
    dqkv[:, :128] = dqt[...].T.astype(BF)
    dqkv[:, 128:] = dkv[...].astype(BF)

    def part(i, _):
        rows = pl.ds(pl.multiple_of(i * 256, 256), 256)
        v = nt(dqkv[rows, :], wsel[...].reshape(1024, 384)).astype(BF)
        dts[pl.ds(2 * i, 2)] = v.reshape(2, 128, 1024)
        return 0

    lax.fori_loop(0, 4, part, 0)
    dt_cps = [go(dts.at[t], dtr.at[me], d) for d, t in peers]

    def rows_of(i, _):
        v = nn(tall_t[pl.ds(pl.multiple_of(i * 256, 256), 256), :], dqkv[...])
        gq[pl.ds(2 * i, 2)] = v.astype(BF).reshape(2, 2, 64, 384)
        return 0

    lax.fori_loop(0, 4, rows_of, 0)
    c_cp = go(gq.at[:, 1 - p.c], gq_c, p.to(dc=1))

    cols = jnp.sum(dqkv[...].astype(F32), axis=0, keepdims=True)
    small_src[...] = small[...]
    small_src[me // 4, me % 4, 0, 0:1, 0:128] = cols[:, :128]
    small_src[me // 4, me % 4, 0, 1:2, 0:128] = cols[:, 256:]
    small_swap = s.remote(small_src, small_in, p.to(dc=1))
    small_red = Reduce(p, s, "xyz", small_g, small_bufs, small_total)
    advance(queue, 2)
    small_swap.wait_recv()
    small_g[...] = small_src[...] + small_in[...]
    small_red.first()

    c_cp.wait_recv()

    def add_core(i, _):
        gq_c[i] = (gq_c[i].astype(F32) + gq[i, p.c].astype(F32)).astype(BF)
        return 0

    lax.fori_loop(0, 8, add_core, 0)
    x_cp = go(gq_c.at[pl.ds((1 - p.xl) * 4, 4)], gq_x, p.to(dx=1 - 2 * p.xl))
    advance(queue, 3)
    small_red.second()
    x_cp.wait_recv()

    def add_x(i, _):
        gq_x[i] = (gq_x[i].astype(F32) + gq_c[p.xl * 4 + i].astype(F32)).astype(BF)
        return 0

    lax.fori_loop(0, 4, add_x, 0)
    y_cps = [go(gq_x.at[lax.rem(p.y + d, 4)], gq_y.at[d - 1], p.to(dy=d)) for d in (1, 3, 2)]
    advance(queue, 3)
    small_red.third()
    for cp in y_cps:
        cp.wait_recv()
    acc = gq_x[p.y].astype(F32)
    for i in range(3):
        acc = acc + gq_y[i].astype(F32)
    gw[me] = acc.astype(BF)
    gw_cps = [go(gw.at[me], gw.at[me], d) for d, _ in peers]
    advance(queue, 3)
    small_red.share()
    for cp in dt_cps:
        cp.wait_recv()
    dtr[me] = dts[me]
    acc = gsum[...]
    for t in range(8):
        acc = acc + dtr[t].astype(F32)
    grad_tok[...] = acc.astype(BF)
    small_red.spread()
    advance(queue, len(queue))
    for cp in gw_cps:
        cp.wait_recv()
    small_red.done()
    prod.finish()
    small_red.finish()
    small_swap.wait_send()
    for cp in sent:
        cp.wait_send()


def attend_backward(pairs, small, gctx, gsum, tall_t, wsel, qkv, lse):
    lefts = [pairs[m][0].reshape(2, 4, 2, ROWS[m], 128) for m in GRAD_NAMES]
    rights = [pairs[m][1] for m in GRAD_NAMES]
    scratch = [pltpu.VMEM((2, 4, ROWS[m], 256), BF) for m in GRAD_NAMES]
    scratch += [pltpu.VMEM((256, COLS[m]), BF) for m in GRAD_NAMES]
    scratch += [pltpu.VMEM(SMALL_SHAPE, F32)] * 3
    scratch += [pltpu.VMEM(x, F32) for x in reduce_shapes("xyz", 8, 256)]
    scratch += piece_scratch(PIECES)
    scratch += [
        pltpu.VMEM((8, 128, 128), BF),
        pltpu.VMEM((128, 1024), BF),
        pltpu.VMEM((128, 1024), F32),
        pltpu.VMEM((1024, 256), F32),
        pltpu.VMEM((1024, 384), BF),
        pltpu.VMEM((8, 2, 64, 384), BF),
        pltpu.VMEM((8, 64, 384), BF),
        pltpu.VMEM((4, 64, 384), BF),
        pltpu.VMEM((3, 64, 384), BF),
        pltpu.VMEM((8, 128, 1024), BF),
        pltpu.VMEM((8, 128, 1024), BF),
    ]
    scratch += [pltpu.SemaphoreType.DMA((250,)), pltpu.SemaphoreType.DMA((250,))]
    k = len(GRAD_NAMES)
    out = pl.pallas_call(
        backward_kernel,
        out_shape=[jax.ShapeDtypeStruct((4, ROWS[m] // 4, COLS[m]), BF) for m in GRAD_NAMES]
        + [
            jax.ShapeDtypeStruct((4, 8, 256), F32),
            jax.ShapeDtypeStruct((128, 1024), BF),
            jax.ShapeDtypeStruct((8, 64, 384), BF),
        ],
        in_specs=[ANYWHERE] * (2 * k) + [INSIDE, ANYWHERE] + [INSIDE] * 5,
        out_specs=[INSIDE] * (k + 3),
        scratch_shapes=scratch,
        compiler_params=pltpu.CompilerParams(
            collective_id=2, has_side_effects=True, vmem_limit_bytes=63 * 2**20
        ),
        name="attend_backward",
    )(*lefts, *rights, small, gctx, gsum, tall_t, wsel, qkv, lse)
    grads = {m: o.reshape(ROWS[m], COLS[m]).astype(F32) for m, o in zip(GRAD_NAMES, out)}
    gw = out[k + 2].reshape(8, 64, 3, 128).transpose(1, 2, 0, 3)
    grads["qkv"] = gw.reshape(64, 3072).astype(F32)
    return grads, out[k], out[k + 1]


def on_device(
    tokens,
    cotangent,
    w_qkv,
    bias_q,
    bias_v,
    w_out,
    bias_out,
    gain_one,
    shift_one,
    w_up,
    bias_up,
    w_down,
    bias_down,
    gain_two,
    shift_two,
):
    num_seqs, slice_len, model_width = tokens.shape
    row_count = num_seqs * slice_len
    inputs = tokens.reshape(row_count, model_width)
    own = dict(
        bias_q=bias_q,
        bias_v=bias_v,
        bias_out=bias_out,
        gain_one=gain_one,
        shift_one=shift_one,
        bias_down=bias_down,
        gain_two=gain_two,
        shift_two=shift_two,
    )
    vectors = jnp.stack([own[k] for k in VECTORS]).astype(F32)
    small, full_out, full_up, full_down, tall, wsel, qkv, lse, context_tokens = attend_forward(
        inputs, w_qkv, vectors, bias_up.astype(F32).reshape(1, 256), [w_out, w_up, w_down]
    )
    output, grad_context, grad_sum_one, l_down, l_up, l_out, r_down, r_up, r_out, sums = run_middle(
        inputs,
        context_tokens,
        cotangent.reshape(row_count, model_width),
        small,
        full_out,
        full_up,
        full_down,
    )
    grads, total, grad_inputs = attend_backward(
        {
            "down": (l_down, r_down),
            "up": (l_up, r_up),
            "out": (l_out, r_out),
        },
        sums,
        grad_context,
        grad_sum_one,
        tall.reshape(1024, model_width).T,
        wsel,
        qkv,
        lse,
    )
    core = lax.axis_index("fsdp") % 2
    mine = lax.dynamic_slice(total, (0, 0, core * 64), (1, 8, 64))
    res = {k: mine[0, r] for r, k in enumerate(VECTORS)}
    res["bias_up"] = lax.dynamic_slice(total, (1, core, 0), (1, 1, 256)).reshape(256)
    return (
        output.reshape(tokens.shape),
        grad_inputs.reshape(tokens.shape),
        grads["qkv"],
        res["bias_q"],
        res["bias_v"],
        grads["out"],
        res["bias_out"],
        res["gain_one"],
        res["shift_one"],
        grads["up"],
        res["bias_up"],
        grads["down"],
        res["bias_down"],
        res["gain_two"],
        res["shift_two"],
    )


def solution(mesh):
    rows, vector = P("fsdp", None), P("fsdp")
    block = P("fsdp", "sp", None)
    params = (rows, vector, vector, rows, vector, vector, vector)
    params += (rows, vector, rows, vector, vector, vector)
    return jax.shard_map(
        on_device,
        mesh=mesh,
        in_specs=(block, block) + params,
        out_specs=(block, block) + params,
        check_vma=False,
    )
```

profile of v0, /device:TPU:0, one launch (start us, length us, event | category | flops | bytes accessed | tf_op | source)
XLA Modules:
  0.0 250.0 jit_solution(2129392370940128386)
XLA Ops:
  0.6 0.8 stack.35
  1.4 0.7 reshape.112
  2.1 0.0 copy-start.1
  2.1 0.9 copy-done.1
  3.1 0.0 copy-start.4
  3.1 1.0 copy-done.4
  4.1 0.0 copy-start.5
  4.1 1.0 copy-done.5
  5.1 0.0 copy-start.6
  5.1 1.0 copy-done.6
  6.1 0.0 copy-start.9
  6.1 0.9 copy-done.9
  7.0 87.6 %attend_forward.1 = (f32[2,4,2,1,16,256]{5,4,3,2,1,0:T(8,128)S(1)}, bf16[2,4,2,4,16,1024]{5,4,3,2,1,0:T(8,128)(2,1)S(1)}, bf16[2,4,2,4,16,4096]{5,4,3,2,1,0:T(8,...) custom-call(bf16[128,1024]{1,0:T(8,128)(2,1)S(1)} %bitcast.59, ...), custom_call_target="tpu_custom_call" | custom-call | tf_op jit(solution)/shard_map/attend_forward/pallas_call | solution.py:461
  94.7 0.0 copy-start
  94.7 1.3 copy-done
  96.0 0.0 copy-start.2
  96.0 0.9 copy-done.2
  96.9 0.0 copy-start.3
  96.9 0.9 copy-done.3
  97.8 0.0 copy-start.7
  97.8 0.7 copy-done.7
  98.5 0.0 copy-start.8
  98.5 0.7 copy-done.8
  99.2 0.0 copy-start.10
  99.2 0.6 copy-done.10
  99.8 19.3 %middle.1 = (bf16[128,1024]{1,0:T(8,128)(2,1)}, bf16[128,1024]{1,0:T(8,128)(2,1)}, f32[128,1024]{1,0:T(8,128)}, bf16[8,2,256,128]{3,2,1,0:T(8,128)(2,1)}, bf16[8...) custom-call(bf16[128,1024]{1,0:T(8,128)(2,1)} %bitcast.58, ...), custom_call_target="tpu_custom_call" | custom-call | tf_op jit(solution)/shard_map/middle/pallas_call | solution.py:733
  119.1 2.6 %copy.35 = bf16[1024,1024]{0,1:T(8,128)(2,1)} copy(bf16[1024,1024]{1,0:T(8,128)(2,1)S(1)} %bitcast.57) | data formatting | bytes 4194304 | tf_op jit(solution)/shard_map/reshape | solution.py:1028
  121.7 119.1 %attend_backward.1 = (bf16[4,64,1024]{2,1,0:T(8,128)(2,1)}, bf16[4,16,4096]{2,1,0:T(8,128)(2,1)}, bf16[4,16,1024]{2,1,0:T(8,128)(2,1)}, f32[4,8,256]{2,1,0:T(8,1...) custom-call(bf16[2,4,2,256,128]{4,3,2,1,0:T(8,128)(2,1)} %bitcast.69, bf16[2,4,2,64,128]{4,3,2,1,0:T(8,128)(2,1)} %bitcast.72, ...), custom_call_target="tpu_custom_call" | custom-call | tf_op jit(solution)/shard_map/attend_backward/pallas_call | solution.py:954
  240.8 0.0 copy-start.12
  240.9 1.4 reshape.118
  242.3 0.0 copy-start.11
  242.3 0.5 copy.34
  242.8 0.0 copy-start.14
  242.8 1.0 copy.38
  243.8 0.0 copy-start.13
  243.8 0.0 copy-done.12
  243.8 1.1 bitcast_convert_fusion
  244.9 0.0 copy-done.11
  244.9 1.1 bitcast_convert_fusion.1
  246.0 0.0 copy-done.14
  246.0 0.7 bitcast_convert_fusion.2
  246.8 0.8 constant_dynamic-slice_fusion.1
  247.5 0.5 slice_bitcast_fusion
  248.1 1.3 constant_dynamic-slice_fusion
  249.3 0.0 copy-done.13
  249.3 0.7 copy.40
  (1 shorter events, 0.0 us)
Async XLA Ops:
  2.1 0.9 copy-start.1
  3.1 1.0 copy-start.4
  4.1 1.0 copy-start.5
  5.1 1.0 copy-start.6
  6.1 0.9 copy-start.9
  94.7 1.3 copy-start
  96.0 0.9 copy-start.2
  96.9 0.9 copy-start.3
  97.8 0.7 copy-start.7
  98.5 0.7 copy-start.8
  99.2 0.6 copy-start.10
  240.8 3.0 %copy-start.12 = (bf16[4,64,1024]{2,1,0:T(8,128)(2,1)S(1)}, bf16[4,64,1024]{2,1,0:T(8,128)(2,1)}, u32[]{:S(2)}) copy-start(bf16[4,64,1024]{2,1,0:T(8,128)(2,1)} %get-tuple-element.64) | copy-start | bytes 1572868
  242.3 2.6 %copy-start.11 = (bf16[4,16,4096]{2,1,0:T(8,128)(2,1)S(1)}, bf16[4,16,4096]{2,1,0:T(8,128)(2,1)}, u32[]{:S(2)}) copy-start(bf16[4,16,4096]{2,1,0:T(8,128)(2,1)} %get-tuple-element.63) | copy-start | bytes 1572868
  242.8 3.3 %copy-start.14 = (bf16[4,16,1024]{2,1,0:T(8,128)(2,1)S(1)}, bf16[4,16,1024]{2,1,0:T(8,128)(2,1)}, u32[]{:S(2)}) copy-start(bf16[4,16,1024]{2,1,0:T(8,128)(2,1)} %get-tuple-element.62) | copy-start | bytes 393220
  243.8 5.5 %copy-start.13 = (bf16[128,1024]{1,0:T(8,128)(2,1)S(1)}, bf16[128,1024]{1,0:T(8,128)(2,1)}, u32[]{:S(2)}) copy-start(bf16[128,1024]{1,0:T(8,128)(2,1)} %get-tuple-element.59) | copy-start | bytes 786436
where the time goes:
time: 251 us; the launch traced here: 250 us
  Pallas kernels  226 us (90%)
  local copies, waits for them, and re-layouts  19.7 us (8%)
  other arithmetic  3.6 us (1%)
    pallas_call x1, Pallas kernels, attend_backward(): pl.pallas_call(backward_kernel, out_shape=[jax.ShapeDtypeStruct((4, ROWS[...  119 us
    pallas_call x1, Pallas kernels, attend_forward(): pl.pallas_call(forward_kernel, out_shape=shapes, in_specs=[ANYWHERE] * 2...  87.6 us
    pallas_call x1, Pallas kernels, run_middle(): pl.pallas_call(middle_kernel, out_shape=[b(128, 1024), b(128, 1024), f(12...  19.3 us
    unnamed x32, local copies, waits for them, and re-layouts  11.8 us

commit v1 on v0

--- a/solution.py
+++ b/solution.py
@@ -267,23 +267,15 @@
     return out
 
 
-def run_pipe(steps, offsets, count):
-    for t in range(count + max(offsets)):
-        for step, d in zip(steps, offsets):
-            if 0 <= t - d < count:
-                step(t - d)
-
-
 ROWS = {"small": 16, "out": 64, "up": 64, "down": 256}
 COLS = {"small": 256, "out": 1024, "up": 4096, "down": 1024}
 GATHER_NAMES = ("small", "out", "up", "down")
 GATHER_PARTS = (
     ("small", 0, 256, False),
     ("out", 0, 1024, False),
-    ("up", 0, 1024, True),
-    ("up", 1024, 1024, False),
+    ("up", 0, 2048, False),
     ("up", 2048, 1024, True),
-    ("up", 3072, 1024, False),
+    ("up", 3072, 1024, True),
     ("down", 0, 512, False),
     ("down", 512, 512, False),
 )
@@ -363,7 +355,8 @@
         for j in range(3)
     ]
     own_tok = s.local(tok, tall.at[me])
-    tok_cps = [go(tok, tall.at[me], d) for d, _ in peers]
+    across = go(tok, tall.at[me], p.to(dx=2))
+    tok_cps = [go(tok, tall.at[me], p.to(dz=d)) for d in (1, 3, 2)]
     parts = [Gather(p, s, ins[m], outs[m], lo, n, quarters) for m, lo, n, quarters in GATHER_PARTS]
     parts[0].start()
     for cp in pick:
@@ -385,6 +378,9 @@
         cp.wait_recv()
     column = wsel.at[p.xl, :, p.c]
     wx = go(column, column, p.to(dx=1 - 2 * p.xl))
+    across.wait_recv()
+    far = tall.at[(1 - p.xh) * 4 + p.z]
+    tok_cps += [go(far, far, p.to(dz=d)) for d in (1, 3, 2)]
     parts[0].stage_x()
     advance(queue, 1)
     wx.wait_recv()
@@ -474,7 +470,7 @@
             pltpu.SemaphoreType.DMA((200,)),
         ],
         compiler_params=pltpu.CompilerParams(
-            collective_id=1, has_side_effects=True, vmem_limit_bytes=40 * 2**20
+            collective_id=1, has_side_effects=True, vmem_limit_bytes=62 * 2**20
         ),
         name="attend_forward",
     )(tokens, w_qkv, vectors, bias_up, *ins)
@@ -485,77 +481,96 @@
 SMALL_SHAPE = (2, 4, 4, 8, 256)
 
 
-class Products:
-    def __init__(self, place, copies, left, right, both_left, both_right, totals, pieces, g, bufs):
-        self.p, self.s = place, copies
-        self.left, self.right = left, right
-        self.both_left, self.both_right = both_left, both_right
-        self.pieces, self.g = pieces, g
-        self.swaps, self.ready = {}, set()
-        self.red = [
-            Reduce(place, copies, o, gi, b, totals[m].at[:, :, pl.ds(lo, n)])
-            for (m, lo, n, o), gi, b in zip(pieces, g, bufs)
+class ReduceTwo(Reduce):
+    def __init__(self, place, copies, order, g, bufs, total):
+        self.p, self.s, self.order, self.g = place, copies, order, g
+        self.r1, self.s1, self.r2 = bufs
+        self.tot = total
+        self.n = g.shape[-1]
+        self.sent = []
+
+    def pick(self, ref, i, v):
+        if self.order[i] == "x":
+            rest = [slice(None)] * (len(ref.shape) - 2)
+            return ref.at[(lax.rem(v, 2),) + tuple(rest) + (self.half(v // 2),)]
+        return ref.at[:, v] if i == 0 else ref.at[v]
+
+    def share(self):
+        mine = self.tot.at[self.p.z, :, self.half(self.p.xh)]
+        self.add(1, self.s1, self.r2, mine, self.c2)
+        self.c4 = self.go(mine, mine, dx=2)
+
+
+def reduce_two_shapes(order, rows, n):
+    if order[0] == "x":
+        return [(3, 4, rows, n // 2), (4, rows, n // 2), (3, rows, n // 2)]
+    return [(3, 2, rows, n), (2, rows, n), (3, rows, n // 2)]
+
+
+class Tokens:
+    def __init__(self, place, copies, axis, left, right, both_left, both_right):
+        self.p, self.s, self.axis = place, copies, axis
+        self.left, self.right, self.bl, self.br = left, right, both_left, both_right
+        self.sent, self.cps, self.own = [], [], []
+
+    def lanes(self, ref, at, n):
+        return ref.at[(slice(None),) * (len(ref.shape) - 1) + (pl.ds(at, n),)]
+
+    def sources(self, t):
+        if self.axis == "y":
+            return self.left.at[:, t], self.right
+        return self.left, self.right.at[:, pl.ds(pl.multiple_of(t * 1024, 128), 1024)]
+
+    def place(self):
+        me = self.p.y if self.axis == "y" else self.p.z
+        return me, pl.multiple_of(me * 128, 128)
+
+    def send(self, side, steps=(1, 3, 2, 0)):
+        me, slot = self.place()
+        dst = self.lanes(self.bl, slot, 128) if side == 0 else self.br.at[pl.ds(slot, 128)]
+        for k in steps:
+            src = self.sources(lax.rem(me + k, 4))[side]
+            if k == 0:
+                self.own.append(self.s.local(src, dst))
+                continue
+            cp = self.s.remote(src, dst, self.p.to(**{"d" + self.axis: k}))
+            self.cps.append(cp)
+            self.sent.append(cp)
+
+    def rows_of(self, ref, c):
+        return ref.at[:, c] if self.axis == "y" else ref.at[:, :, c]
+
+    def swap(self):
+        p, s = self.p, self.s
+        for cp in self.own:
+            cp.wait()
+        for cp in self.cps:
+            cp.wait_recv()
+        far = self.rows_of(self.bl, 1 - p.c)
+        self.cores = [
+            s.remote(self.lanes(far, 0, 512), self.lanes(far, 512, 512), p.to(dc=1)),
+            s.remote(self.br.at[pl.ds(0, 512)], self.br.at[pl.ds(512, 512)], p.to(dc=1)),
         ]
-
-    def swap(self, m):
-        p, s = self.p, self.s
-        here = [
-            s.local(self.left[m].at[:, :, p.c], self.both_left[m].at[:, :, :, pl.ds(0, 128)]),
-            s.local(self.right[m], self.both_right[m].at[pl.ds(0, 128)]),
-        ]
-        there = [
-            s.remote(
-                self.left[m].at[:, :, 1 - p.c],
-                self.both_left[m].at[:, :, :, pl.ds(128, 128)],
-                p.to(dc=1),
-            ),
-            s.remote(self.right[m], self.both_right[m].at[pl.ds(128, 128)], p.to(dc=1)),
-        ]
-        self.swaps[m] = (here, there)
-
-    def begin(self, i):
-        m, lo, n, _ = self.pieces[i]
-        if m not in self.ready:
-            for cp in self.swaps[m][0]:
-                cp.wait()
-            for cp in self.swaps[m][1]:
-                cp.wait_recv()
-            self.ready.add(m)
-        left, right, g = self.both_left[m], self.both_right[m], self.g[i]
-        rows = left.shape[2]
-        tile = min(512, n)
-
-        def body(j, _):
-            b, t = j // (n // tile), lax.rem(j, n // tile)
-            c0 = pl.multiple_of(lo + t * tile, tile)
-            v = jnp.dot(
-                left[b].reshape(4 * rows, 256),
-                right[:, pl.ds(c0, tile)],
-                preferred_element_type=F32,
-            ).astype(BF)
-            g[b, :, :, :, pl.ds(pl.multiple_of(t * tile, tile), tile)] = v.reshape(
-                4, 4, rows // 4, tile
-            )
+        self.sent += self.cores
+
+    def ready(self):
+        for cp in self.cores:
+            cp.wait_recv()
+
+    def multiply(self, lo, g):
+        n = g.shape[-1]
+
+        def body(b, _):
+            left = self.bl[b, self.p.c] if self.axis == "y" else self.bl[b, :, self.p.c]
+            v = nn(left.reshape(4 * g.shape[2], 1024), self.br[:, lo : lo + n])
+            g[b] = v.astype(BF).reshape(4, g.shape[2], n)
             return 0
 
-        lax.fori_loop(0, 2 * (n // tile), body, 0)
-        self.red[i].first()
+        lax.fori_loop(0, 2, body, 0)
 
     def finish(self):
-        for r in self.red:
-            r.finish()
-        for m in self.swaps:
-            for cp in self.swaps[m][1]:
-                cp.wait_send()
-
-
-def piece_scratch(pieces):
-    sc = []
-    for m, _, n, o in pieces:
-        q = ROWS[m] // 4
-        sc.append(pltpu.VMEM((2, 4, 4, q, n), BF))
-        sc += [pltpu.VMEM(x, BF) for x in reduce_shapes(o, q, n)]
-    return sc
+        for cp in self.sent:
+            cp.wait_send()
 
 
 VECTORS = (
@@ -610,6 +625,8 @@
     hat1,
     base,
     acc,
+    toks,
+    place,
 ):
     for r, name in enumerate(VECTORS):
         for j in range(8):
@@ -635,8 +652,10 @@
     base[...] = normed
     low = normed.astype(BF)
     rights["low"][...] = low
-    lefts["up"][...] = normed.T.astype(BF).reshape(8, 2, 64, 128)
-    lefts["out"][...] = ctx[...].astype(F32).T.astype(BF).reshape(8, 2, 64, 128)
+    lefts["up"][...] = normed.T.astype(BF).reshape(2, 4, 2, 64, 128)
+    lefts["out"][...] = ctx[...].astype(F32).T.astype(BF).reshape(2, 4, 2, 64, 128)
+    toks["up"].send(0)
+    toks["out"].send(0)
     acc[...] = jnp.zeros_like(acc)
 
     def up(t, _):
@@ -646,12 +665,13 @@
         cdf = 0.5 * (1.0 + lax.erf(pre * root_half))
         slope[:, cols] = cdf + pre * jnp.exp(-0.5 * pre * pre) * inv_root_two_pi
         act = pre * cdf
-        lefts["down"][t] = act.T.astype(BF).reshape(2, 256, 128)
+        lefts["down"][t // 4, lax.rem(t, 4)] = act.T.astype(BF).reshape(2, 256, 128)
         wait_down(t)
         acc[...] += nn(act.astype(BF), w_down[t])
         return 0
 
     lax.fori_loop(0, 8, up, 0)
+    toks["down"].send(0)
     hat2, inv2 = ln_rows(base[...] + acc[...] + row["bias_down"])
     output[...] = (hat2 * row["gain_two"] + row["shift_two"]).astype(BF)
     dy = cot[...].astype(F32)
@@ -661,9 +681,11 @@
     acc[...] = gs2
     ffn = gs2.astype(BF)
     rights["down"][...] = ffn
+    toks["down"].send(1)
     put("bias_down", col_sum(ffn.astype(F32)))
 
-    def back(t, _):
+    def back(k, j, _):
+        t = 2 * lax.rem(place.z + k, 4) + j
         cols = pl.ds(pl.multiple_of(t * 512, 512), 512)
         pre = (nt(rights["down"][...], w_down[t]) * slope[:, cols]).astype(BF)
         rights["up"][:, cols] = pre
@@ -673,7 +695,9 @@
         acc[...] += nt(pre, w_up[t])
         return 0
 
-    lax.fori_loop(0, 8, back, 0)
+    for k in (1, 3, 2, 0):
+        lax.fori_loop(0, 2, functools.partial(back, k), 0)
+        toks["up"].send(1, (k,))
     gn = acc[...]
     hat = hat1[...]
     put("gain_one", col_sum(gn * hat))
@@ -682,90 +706,21 @@
     gsum[...] = gs1
     gb = gs1.astype(BF)
     rights["out"][...] = gb
+    toks["out"].send(1)
     put("bias_out", col_sum(gb.astype(F32)))
     gctx[...] = nt(gb, w_out[...]).astype(BF)
 
 
-def middle_kernel(
-    tok, ctx, cot, small_h, out_h, up_h, down_h,
-    output, gctx, gsum, l_down, l_up, l_out, r_down, r_up, r_out, small,
-    small_v, w_out, w_up, w_down, low, vec, bup, slope, hat1, base, acc, sem,
-):
-    cps = [pltpu.make_async_copy(small_h, small_v, sem.at[0])]
-    cps += [pltpu.make_async_copy(out_h, w_out, sem.at[1])]
-    ups = [
-        pltpu.make_async_copy(up_h.at[:, pl.ds(t * 512, 512)], w_up.at[t], sem.at[2 + t])
-        for t in range(8)
-    ]
-    downs = [
-        pltpu.make_async_copy(down_h.at[pl.ds(t * 512, 512)], w_down.at[t], sem.at[10 + t])
-        for t in range(8)
-    ]
-    for cp in cps:
-        cp.start()
-    for a, b in zip(ups, downs):
-        a.start()
-        b.start()
-    cps[0].wait()
-
-    def wait_up(t):
-        pltpu.make_async_copy(up_h.at[:, pl.ds(0, 512)], w_up.at[t], sem.at[2 + t]).wait()
-
-    def wait_down(t):
-        pltpu.make_async_copy(down_h.at[pl.ds(0, 512)], w_down.at[t], sem.at[10 + t]).wait()
-
-    middle(
-        tok, ctx, cot, small_v, cps[1].wait, wait_up, wait_down, w_out, w_up, w_down,
-        output, gctx, gsum,
-        {"down": l_down, "up": l_up, "out": l_out},
-        {"down": r_down, "up": r_up, "out": r_out, "low": low},
-        small, vec, bup, slope, hat1, base, acc,
-    )
-
-
-def run_middle(tok, ctx, cot, small_full, full_out, full_up, full_down):
-    def b(*s):
-        return jax.ShapeDtypeStruct(s, BF)
-
-    def f(*s):
-        return jax.ShapeDtypeStruct(s, F32)
-
-    return pl.pallas_call(
-        middle_kernel,
-        out_shape=[b(128, 1024), b(128, 1024), f(128, 1024)]
-        + [b(8, 2, 256, 128), b(8, 2, 64, 128), b(8, 2, 64, 128)]
-        + [b(128, 1024), b(128, 4096), b(128, 1024), f(2, 4, 4, 8, 256)],
-        in_specs=[INSIDE] * 3 + [ANYWHERE] * 4,
-        out_specs=[INSIDE] * 10,
-        scratch_shapes=[
-            pltpu.VMEM((2, 4, 2, 1, 16, 256), F32),
-            pltpu.VMEM((1024, 1024), BF),
-            pltpu.VMEM((8, 1024, 512), BF),
-            pltpu.VMEM((8, 512, 1024), BF),
-            pltpu.VMEM((128, 1024), BF),
-            pltpu.VMEM((8, 1024), F32),
-            pltpu.VMEM((8, 4096), F32),
-            pltpu.VMEM((128, 4096), F32),
-            pltpu.VMEM((128, 1024), F32),
-            pltpu.VMEM((128, 1024), F32),
-            pltpu.VMEM((128, 1024), F32),
-            pltpu.SemaphoreType.DMA((18,)),
-        ],
-        compiler_params=pltpu.CompilerParams(vmem_limit_bytes=56 * 2**20),
-        name="middle",
-    )(tok, ctx, cot, small_full, full_out, full_up, full_down)
-
-
+GRAD_NAMES = ("down", "up", "out")
+GRAD_AXIS = {"down": "y", "up": "z", "out": "y"}
+PIECE_ROWS = {"down": 64, "up": 64, "out": 16}
 PIECES = (
-    ("down", 0, 512, "yzx"),
-    ("up", 0, 1024, "xyz"),
-    ("down", 512, 512, "zxy"),
-    ("up", 1024, 1024, "yzx"),
-    ("up", 2048, 1024, "zxy"),
-    ("up", 3072, 1024, "xyz"),
-    ("out", 0, 1024, "yzx"),
+    ("down", 0, 512, "xz"),
+    ("down", 512, 512, "zx"),
+    ("up", 0, 512, "yx"),
+    ("up", 512, 512, "xy"),
+    ("out", 0, 1024, "zx"),
 )
-GRAD_NAMES = ("down", "up", "out")
 
 
 def backward_kernel(*refs):
@@ -777,11 +732,13 @@
         return head
 
     k = len(GRAD_NAMES)
+    tok, ctx, cot, small_h, out_h, up_h, down_h, tall_t, wsel, qkv, lse = take(11)
+    totals = dict(zip(GRAD_NAMES, take(k)))
+    small_total, grad_tok, gw, output = take(4)
+    small_v, w_out, w_up, w_down, low, vec, bup, slope, hat1, base, acc, sem = take(12)
+    gctx, gsum = take(2)
     left = dict(zip(GRAD_NAMES, take(k)))
     right = dict(zip(GRAD_NAMES, take(k)))
-    small, gctx, gsum, tall_t, wsel, qkv, lse = take(7)
-    totals = dict(zip(GRAD_NAMES, take(k)))
-    small_total, grad_tok, gw = take(3)
     both_left = dict(zip(GRAD_NAMES, take(k)))
     both_right = dict(zip(GRAD_NAMES, take(k)))
     small_src, small_in, small_g = take(3)
@@ -789,8 +746,23 @@
     g, bufs = [], []
     for _ in PIECES:
         g += take(1)
-        bufs.append(take(5))
-    do, kt, dqt, dkv, dqkv, gq, gq_c, gq_x, gq_y, dts, dtr = take(11)
+        bufs.append(take(3))
+    do, kt, dqt, dkv, dqkv, gq, gq_c, gq_x, gq_y = take(9)
+    dts, dtx, dtxr, dtz, dtz_s, dtzr = take(6)
+    vec_cp = pltpu.make_async_copy(small_h, small_v, sem.at[0])
+    out_cp = pltpu.make_async_copy(out_h, w_out, sem.at[1])
+    vec_cp.start()
+    out_cp.start()
+    for t in range(8):
+        pltpu.make_async_copy(up_h.at[:, pl.ds(t * 512, 512)], w_up.at[t], sem.at[2 + t]).start()
+        pltpu.make_async_copy(down_h.at[pl.ds(t * 512, 512)], w_down.at[t], sem.at[10 + t]).start()
+
+    def wait_up(t):
+        pltpu.make_async_copy(up_h.at[:, pl.ds(0, 512)], w_up.at[t], sem.at[2 + t]).wait()
+
+    def wait_down(t):
+        pltpu.make_async_copy(down_h.at[pl.ds(0, 512)], w_down.at[t], sem.at[10 + t]).wait()
+
     p, s = Place(), Copies(*refs)
     me = p.xh * 4 + p.z
     peers = sp_peers(p)
@@ -805,61 +777,105 @@
         sent.append(cp)
         return cp
 
+    toks = {
+        m: Tokens(p, s, GRAD_AXIS[m], left[m], right[m], both_left[m], both_right[m])
+        for m in GRAD_NAMES
+    }
+    vec_cp.wait()
+    middle(
+        tok,
+        ctx,
+        cot,
+        small_v,
+        out_cp.wait,
+        wait_up,
+        wait_down,
+        w_out,
+        w_up,
+        w_down,
+        output,
+        gctx,
+        gsum,
+        left,
+        dict(right, low=low),
+        small_src,
+        vec,
+        bup,
+        slope,
+        hat1,
+        base,
+        acc,
+        toks,
+        p,
+    )
     do_cps = [
         go(gctx.at[:, pl.ds(pl.multiple_of(t * 128, 128), 128)], do.at[me], d) for d, t in peers
     ]
     do_own = s.local(gctx.at[:, pl.ds(pl.multiple_of(me * 128, 128), 128)], do.at[me])
-    prod = Products(p, s, left, right, both_left, both_right, totals, PIECES, g, bufs)
-    for m in GRAD_NAMES:
-        prod.swap(m)
+    toks["down"].swap()
+    red = [
+        ReduceTwo(p, s, o, gi, b, totals[m].at[:, :, pl.ds(lo, n)])
+        for (m, lo, n, o), gi, b in zip(PIECES, g, bufs)
+    ]
     kt[...] = qkv[:, 128:256].astype(F32).T.astype(BF)
-    red = prod.red
-    n = len(PIECES)
-    for i in range(n):
-        prod.begin(i)
-    queue = flat_pipe(
-        (
-            lambda i: red[i].second(),
-            lambda i: red[i].third(),
-            lambda i: red[i].share(),
-            lambda i: red[i].spread(),
-            lambda i: red[i].done(),
-        ),
-        (0, 2, 4, 5, 6),
-        n,
-    )
+    toks["up"].swap()
+    ready = set()
+
+    def begin(i):
+        m, lo, _, _ = PIECES[i]
+        if m not in ready:
+            toks[m].ready()
+            ready.add(m)
+        toks[m].multiply(lo, g[i])
+        red[i].first()
+
+    begin(0)
+    begin(1)
     do_own.wait()
     for cp in do_cps:
         cp.wait_recv()
     dkv[...] = jnp.zeros_like(dkv)
+
+    def head_block(b, h):
+        rows = pl.ds(b * 256, 256)
+        lanes = slice(64 * h, 64 * h + 64)
+        keys = qkv[:, 128 + 64 * h : 192 + 64 * h]
+        vals = qkv[:, 256 + 64 * h : 320 + 64 * h]
+        q = qkv[rows, lanes]
+        dob = do[2 * b : 2 * b + 2].reshape(256, 128)[:, lanes]
+        probs = jnp.exp(nt(keys, q) * 0.125 - lse[h : h + 1, rows])
+        dp = nt(vals, dob)
+        inner = jnp.sum(probs * dp, axis=0, keepdims=True)
+        ds = (probs * (dp - inner)).astype(BF)
+        dqt[lanes, rows] = nn(kt[lanes, :], ds) * 0.125
+        dkv[:, lanes] += nn(ds, q) * 0.125
+        dkv[:, 128 + 64 * h : 192 + 64 * h] += nn(probs.astype(BF), dob)
+
     for b in range(4):
-        rows = pl.ds(b * 256, 256)
         for h in range(2):
-            lanes = slice(64 * h, 64 * h + 64)
-            keys = qkv[:, 128 + 64 * h : 192 + 64 * h]
-            vals = qkv[:, 256 + 64 * h : 320 + 64 * h]
-            q = qkv[rows, lanes]
-            dob = do[2 * b : 2 * b + 2].reshape(256, 128)[:, lanes]
-            probs = jnp.exp(nt(keys, q) * 0.125 - lse[h : h + 1, rows])
-            dp = nt(vals, dob)
-            inner = jnp.sum(probs * dp, axis=0, keepdims=True)
-            ds = (probs * (dp - inner)).astype(BF)
-            dqt[lanes, rows] = nn(kt[lanes, :], ds) * 0.125
-            dkv[:, lanes] += nn(ds, q) * 0.125
-            dkv[:, 128 + 64 * h : 192 + 64 * h] += nn(probs.astype(BF), dob)
-        if b >= 1:
-            advance(queue, 1)
+            head_block(b, h)
+        if b == 0:
+            begin(2)
+            toks["out"].swap()
+        if b == 1:
+            begin(3)
+        if b == 2:
+            begin(4)
     dqkv[:, :128] = dqt[...].T.astype(BF)
     dqkv[:, 128:] = dkv[...].astype(BF)
 
     def part(i, _):
         rows = pl.ds(pl.multiple_of(i * 256, 256), 256)
         v = nt(dqkv[rows, :], wsel[...].reshape(1024, 384)).astype(BF)
-        dts[pl.ds(2 * i, 2)] = v.reshape(2, 128, 1024)
+        dts[i // 2, pl.ds(2 * lax.rem(i, 2), 2)] = v.reshape(2, 128, 1024)
         return 0
 
     lax.fori_loop(0, 4, part, 0)
-    dt_cps = [go(dts.at[t], dtr.at[me], d) for d, t in peers]
+    first, second = pl.ds(0, 512), pl.ds(512, 512)
+    dx_cp = go(dts.at[1 - p.xh, :, :, first], dtx, p.to(dx=2))
+    dz_cps = [
+        go(dts.at[:, lax.rem(p.z + d, 4), :, second], dtz.at[d - 1], p.to(dz=d)) for d in (1, 3, 2)
+    ]
 
     def rows_of(i, _):
         v = nn(tall_t[pl.ds(pl.multiple_of(i * 256, 256), 256), :], dqkv[...])
@@ -868,28 +884,43 @@
 
     lax.fori_loop(0, 4, rows_of, 0)
     c_cp = go(gq.at[:, 1 - p.c], gq_c, p.to(dc=1))
-
     cols = jnp.sum(dqkv[...].astype(F32), axis=0, keepdims=True)
-    small_src[...] = small[...]
     small_src[me // 4, me % 4, 0, 0:1, 0:128] = cols[:, :128]
     small_src[me // 4, me % 4, 0, 1:2, 0:128] = cols[:, 256:]
     small_swap = s.remote(small_src, small_in, p.to(dc=1))
     small_red = Reduce(p, s, "xyz", small_g, small_bufs, small_total)
-    advance(queue, 2)
+
+    c_cp.wait_recv()
+
+    def add_core(i, _):
+        gq_c[i] = (gq_c[i].astype(F32) + gq[i, p.c].astype(F32)).astype(BF)
+        return 0
+
+    lax.fori_loop(0, 8, add_core, 0)
+    x_cp = go(gq_c.at[pl.ds((1 - p.xl) * 4, 4)], gq_x, p.to(dx=1 - 2 * p.xl))
     small_swap.wait_recv()
     small_g[...] = small_src[...] + small_in[...]
     small_red.first()
-
-    c_cp.wait_recv()
-
-    def add_core(i, _):
-        gq_c[i] = (gq_c[i].astype(F32) + gq[i, p.c].astype(F32)).astype(BF)
+    dx_cp.wait_recv()
+
+    def add_far(i, _):
+        dtx[i] = (dtx[i].astype(F32) + dts[p.xh, i, :, 0:512].astype(F32)).astype(BF)
         return 0
 
-    lax.fori_loop(0, 8, add_core, 0)
-    x_cp = go(gq_c.at[pl.ds((1 - p.xl) * 4, 4)], gq_x, p.to(dx=1 - 2 * p.xl))
-    advance(queue, 3)
-    small_red.second()
+    lax.fori_loop(0, 4, add_far, 0)
+    dz2_cps = [go(dtx.at[lax.rem(p.z + d, 4)], dtxr.at[d - 1], p.to(dz=d)) for d in (1, 3, 2)]
+    for cp in dz_cps:
+        cp.wait_recv()
+
+    def add_round(i, _):
+        v = dts[i, p.z, :, 512:1024].astype(F32)
+        for d in range(3):
+            v = v + dtz[d, i].astype(F32)
+        dtz_s[i] = v.astype(BF)
+        return 0
+
+    lax.fori_loop(0, 2, add_round, 0)
+    dx2_cp = go(dtz_s.at[1 - p.xh], dtzr, p.to(dx=2))
     x_cp.wait_recv()
 
     def add_x(i, _):
@@ -898,8 +929,11 @@
 
     lax.fori_loop(0, 4, add_x, 0)
     y_cps = [go(gq_x.at[lax.rem(p.y + d, 4)], gq_y.at[d - 1], p.to(dy=d)) for d in (1, 3, 2)]
-    advance(queue, 3)
-    small_red.third()
+    for i in range(2):
+        red[i].second()
+    small_red.second()
+    for i in range(2, len(PIECES)):
+        red[i].second()
     for cp in y_cps:
         cp.wait_recv()
     acc = gq_x[p.y].astype(F32)
@@ -907,35 +941,66 @@
         acc = acc + gq_y[i].astype(F32)
     gw[me] = acc.astype(BF)
     gw_cps = [go(gw.at[me], gw.at[me], d) for d, _ in peers]
-    advance(queue, 3)
+    small_red.third()
+    for r in red:
+        r.share()
     small_red.share()
-    for cp in dt_cps:
+    for r in red:
+        r.spread()
+    small_red.spread()
+    for cp in dz2_cps:
         cp.wait_recv()
-    dtr[me] = dts[me]
-    acc = gsum[...]
-    for t in range(8):
-        acc = acc + dtr[t].astype(F32)
-    grad_tok[...] = acc.astype(BF)
-    small_red.spread()
-    advance(queue, len(queue))
+    dx2_cp.wait_recv()
+    acc = gsum[:, 0:512] + dtx[p.z].astype(F32)
+    for t in range(3):
+        acc = acc + dtxr[t].astype(F32)
+    grad_tok[:, 0:512] = acc.astype(BF)
+    acc = gsum[:, 512:1024] + dtz_s[p.xh].astype(F32) + dtzr[...].astype(F32)
+    grad_tok[:, 512:1024] = acc.astype(BF)
     for cp in gw_cps:
         cp.wait_recv()
+    for r in red:
+        r.done()
     small_red.done()
-    prod.finish()
+    for r in red:
+        r.finish()
+    for m in GRAD_NAMES:
+        toks[m].finish()
     small_red.finish()
     small_swap.wait_send()
     for cp in sent:
         cp.wait_send()
 
 
-def attend_backward(pairs, small, gctx, gsum, tall_t, wsel, qkv, lse):
-    lefts = [pairs[m][0].reshape(2, 4, 2, ROWS[m], 128) for m in GRAD_NAMES]
-    rights = [pairs[m][1] for m in GRAD_NAMES]
-    scratch = [pltpu.VMEM((2, 4, ROWS[m], 256), BF) for m in GRAD_NAMES]
-    scratch += [pltpu.VMEM((256, COLS[m]), BF) for m in GRAD_NAMES]
+def finish_layer(tok, ctx, cot, small_h, out_h, up_h, down_h, tall_t, wsel, qkv, lse):
+    scratch = [
+        pltpu.VMEM((2, 4, 2, 1, 16, 256), F32),
+        pltpu.VMEM((1024, 1024), BF),
+        pltpu.VMEM((8, 1024, 512), BF),
+        pltpu.VMEM((8, 512, 1024), BF),
+        pltpu.VMEM((128, 1024), BF),
+        pltpu.VMEM((8, 1024), F32),
+        pltpu.VMEM((8, 4096), F32),
+        pltpu.VMEM((128, 4096), F32),
+        pltpu.VMEM((128, 1024), F32),
+        pltpu.VMEM((128, 1024), F32),
+        pltpu.VMEM((128, 1024), F32),
+        pltpu.SemaphoreType.DMA((18,)),
+        pltpu.VMEM((128, 1024), BF),
+        pltpu.VMEM((128, 1024), F32),
+    ]
+    scratch += [pltpu.VMEM((2, 4, 2, ROWS[m], 128), BF) for m in GRAD_NAMES]
+    scratch += [pltpu.VMEM((128, COLS[m]), BF) for m in GRAD_NAMES]
+    scratch += [
+        pltpu.VMEM((2, 2, ROWS[m], 1024) if GRAD_AXIS[m] == "y" else (2, 4, 2, ROWS[m], 1024), BF)
+        for m in GRAD_NAMES
+    ]
+    scratch += [pltpu.VMEM((1024, 1024), BF) for m in GRAD_NAMES]
     scratch += [pltpu.VMEM(SMALL_SHAPE, F32)] * 3
     scratch += [pltpu.VMEM(x, F32) for x in reduce_shapes("xyz", 8, 256)]
-    scratch += piece_scratch(PIECES)
+    for m, _, n, o in PIECES:
+        scratch.append(pltpu.VMEM((2, 4, PIECE_ROWS[m], n), BF))
+        scratch += [pltpu.VMEM(x, BF) for x in reduce_two_shapes(o, PIECE_ROWS[m], n)]
     scratch += [
         pltpu.VMEM((8, 128, 128), BF),
         pltpu.VMEM((128, 1024), BF),
@@ -946,31 +1011,40 @@
         pltpu.VMEM((8, 64, 384), BF),
         pltpu.VMEM((4, 64, 384), BF),
         pltpu.VMEM((3, 64, 384), BF),
-        pltpu.VMEM((8, 128, 1024), BF),
-        pltpu.VMEM((8, 128, 1024), BF),
+        pltpu.VMEM((2, 4, 128, 1024), BF),
+        pltpu.VMEM((4, 128, 512), BF),
+        pltpu.VMEM((3, 128, 512), BF),
+        pltpu.VMEM((3, 2, 128, 512), BF),
+        pltpu.VMEM((2, 128, 512), BF),
+        pltpu.VMEM((128, 512), BF),
     ]
     scratch += [pltpu.SemaphoreType.DMA((250,)), pltpu.SemaphoreType.DMA((250,))]
     k = len(GRAD_NAMES)
     out = pl.pallas_call(
         backward_kernel,
-        out_shape=[jax.ShapeDtypeStruct((4, ROWS[m] // 4, COLS[m]), BF) for m in GRAD_NAMES]
+        out_shape=[jax.ShapeDtypeStruct((4, PIECE_ROWS[m], 1024), BF) for m in GRAD_NAMES]
         + [
             jax.ShapeDtypeStruct((4, 8, 256), F32),
             jax.ShapeDtypeStruct((128, 1024), BF),
             jax.ShapeDtypeStruct((8, 64, 384), BF),
+            jax.ShapeDtypeStruct((128, 1024), BF),
         ],
-        in_specs=[ANYWHERE] * (2 * k) + [INSIDE, ANYWHERE] + [INSIDE] * 5,
-        out_specs=[INSIDE] * (k + 3),
+        in_specs=[INSIDE] * 3 + [ANYWHERE] * 4 + [INSIDE] * 4,
+        out_specs=[INSIDE] * (k + 4),
         scratch_shapes=scratch,
         compiler_params=pltpu.CompilerParams(
-            collective_id=2, has_side_effects=True, vmem_limit_bytes=63 * 2**20
+            collective_id=2, has_side_effects=True, vmem_limit_bytes=62 * 2**20
         ),
-        name="attend_backward",
-    )(*lefts, *rights, small, gctx, gsum, tall_t, wsel, qkv, lse)
-    grads = {m: o.reshape(ROWS[m], COLS[m]).astype(F32) for m, o in zip(GRAD_NAMES, out)}
+        name="layer_back",
+    )(tok, ctx, cot, small_h, out_h, up_h, down_h, tall_t, wsel, qkv, lse)
+    grads = {
+        "down": out[0].reshape(256, 1024).astype(F32),
+        "up": out[1].transpose(1, 0, 2).reshape(64, 4096).astype(F32),
+        "out": out[2].reshape(64, 1024).astype(F32),
+    }
     gw = out[k + 2].reshape(8, 64, 3, 128).transpose(1, 2, 0, 3)
     grads["qkv"] = gw.reshape(64, 3072).astype(F32)
-    return grads, out[k], out[k + 1]
+    return grads, out[k], out[k + 1], out[k + 3]
 
 
 def on_device(
@@ -1007,7 +1081,7 @@
     small, full_out, full_up, full_down, tall, wsel, qkv, lse, context_tokens = attend_forward(
         inputs, w_qkv, vectors, bias_up.astype(F32).reshape(1, 256), [w_out, w_up, w_down]
     )
-    output, grad_context, grad_sum_one, l_down, l_up, l_out, r_down, r_up, r_out, sums = run_middle(
+    grads, total, grad_inputs, output = finish_layer(
         inputs,
         context_tokens,
         cotangent.reshape(row_count, model_width),
@@ -1015,16 +1089,6 @@
         full_out,
         full_up,
         full_down,
-    )
-    grads, total, grad_inputs = attend_backward(
-        {
-            "down": (l_down, r_down),
-            "up": (l_up, r_up),
-            "out": (l_out, r_out),
-        },
-        sums,
-        grad_context,
-        grad_sum_one,
         tall.reshape(1024, model_width).T,
         wsel,
         qkv,

time: 251 us -> 209 us (0.83)
  Pallas kernels: 226 us -> 191 us
  local copies, waits for them, and re-layouts: 19.7 us -> 12.7 us
    pallas_call x2 -> x1, Pallas kernels: 138 us -> 111 us  [finish_layer(): pl.pallas_call(backward_kernel, out_shape=[jax.ShapeDtypeStruct((4, PIECE...]
    unnamed x32 -> x13, local copies, waits for them, and re-layouts: 11.8 us -> 2.45 us
    pallas_call x1, Pallas kernels: 87.6 us -> 79.9 us  [attend_forward(): pl.pallas_call(forward_kernel, out_shape=shapes, in_specs=[ANYWHERE] * 2...]
where the time goes in v1:
time: 209 us; the launch traced here: 208 us
  Pallas kernels  191 us (91%)
  local copies, waits for them, and re-layouts  12.7 us (6%)
  other arithmetic  3.77 us (2%)
    pallas_call x1, Pallas kernels, finish_layer(): pl.pallas_call(backward_kernel, out_shape=[jax.ShapeDtypeStruct((4, PIECE...  111 us
    pallas_call x1, Pallas kernels, attend_forward(): pl.pallas_call(forward_kernel, out_shape=shapes, in_specs=[ANYWHERE] * 2...  79.9 us

profile of v1, /device:TPU:0, one launch (start us, length us, event | category | flops | bytes accessed | tf_op | source)
XLA Modules:
  0.0 208.5 jit_solution(4940311683395875600)
XLA Ops:
  0.6 0.8 stack.35
  1.4 0.6 convert_element_type.37.refs_2_
  2.0 1.2 reshape.100
  3.3 79.9 %attend_forward.1 = (f32[2,4,2,1,16,256]{5,4,3,2,1,0:T(8,128)}, bf16[2,4,2,4,16,1024]{5,4,3,2,1,0:T(8,128)(2,1)}, bf16[2,4,2,4,16,4096]{5,4,3,2,1,0:T(8,128)(2,1...) custom-call(bf16[128,1024]{1,0:T(8,128)(2,1)} %bitcast.61, ...), custom_call_target="tpu_custom_call" | custom-call | tf_op jit(solution)/shard_map/attend_forward/pallas_call | solution.py:457
  83.1 3.9 %copy.37 = bf16[1024,1024]{0,1:T(8,128)(2,1)} copy(bf16[1024,1024]{1,0:T(8,128)(2,1)} %bitcast.60) | data formatting | bytes 4194304 | tf_op jit(solution)/shard_map/reshape | solution.py:1092
  87.1 111.4 %layer_back.1 = (bf16[4,64,1024]{2,1,0:T(8,128)(2,1)}, bf16[4,64,1024]{2,1,0:T(8,128)(2,1)}, bf16[4,16,1024]{2,1,0:T(8,128)(2,1)}, f32[4,8,256]{2,1,0:T(8,128)},...) custom-call(bf16[128,1024]{1,0:T(8,128)(2,1)} %bitcast.62, ...), custom_call_target="tpu_custom_call" | custom-call | tf_op jit(solution)/shard_map/layer_back/pallas_call | solution.py:1023
  198.4 1.4 reshape.106
  199.8 0.0 copy-start.4
  199.9 0.0 copy-start.1
  199.9 0.5 copy.35
  200.3 1.0 copy.41
  201.3 0.0 copy-start
  201.4 0.8 constant_dynamic-slice_fusion.1
  202.2 0.5 slice_bitcast_fusion
  202.7 0.0 copy-done.4
  202.7 0.7 bitcast_convert_fusion.1
  203.4 0.0 copy-done.1
  203.4 0.1 convert_bitcast_fusion
  203.6 0.0 copy-start.3
  203.6 0.0 copy-start.2
  203.6 1.1 copy.38
  204.7 1.3 constant_dynamic-slice_fusion
  205.9 0.0 copy-done
  205.9 1.1 bitcast_convert_fusion
  207.0 0.0 copy-done.3
  207.0 0.7 copy.44
  207.8 0.0 copy-done.2
  207.8 0.7 copy.45
Async XLA Ops:
  199.8 2.9 %copy-start.4 = (bf16[4,16,1024]{2,1,0:T(8,128)(2,1)S(1)}, bf16[4,16,1024]{2,1,0:T(8,128)(2,1)}, u32[]{:S(2)}) copy-start(bf16[4,16,1024]{2,1,0:T(8,128)(2,1)} %get-tuple-element.44) | copy-start | bytes 393220
  199.9 3.6 %copy-start.1 = (bf16[4,64,1024]{2,1,0:T(8,128)(2,1)S(1)}, bf16[4,64,1024]{2,1,0:T(8,128)(2,1)}, u32[]{:S(2)}) copy-start(bf16[4,64,1024]{2,1,0:T(8,128)(2,1)} %get-tuple-element.45) | copy-start | bytes 1572868
  201.3 4.6 %copy-start = (bf16[4,64,1024]{2,1,0:T(8,128)(2,1)S(1)}, bf16[4,64,1024]{2,1,0:T(8,128)(2,1)}, u32[]{:S(2)}) copy-start(bf16[4,64,1024]{2,1,0:T(8,128)(2,1)} %get-tuple-element.46) | copy-start | bytes 1572868
  203.6 3.5 %copy-start.3 = (bf16[128,1024]{1,0:T(8,128)(2,1)S(1)}, bf16[128,1024]{1,0:T(8,128)(2,1)}, u32[]{:S(2)}) copy-start(bf16[128,1024]{1,0:T(8,128)(2,1)} %get-tuple-element.40) | copy-start | bytes 786436
  203.6 4.2 %copy-start.2 = (bf16[128,1024]{1,0:T(8,128)(2,1)S(1)}, bf16[128,1024]{1,0:T(8,128)(2,1)}, u32[]{:S(2)}) copy-start(bf16[128,1024]{1,0:T(8,128)(2,1)} %get-tuple-element.41) | copy-start | bytes 786436

commit v2 on v1

--- a/solution.py
+++ b/solution.py
@@ -277,7 +277,8 @@
     ("up", 2048, 1024, True),
     ("up", 3072, 1024, True),
     ("down", 0, 512, False),
-    ("down", 512, 512, False),
+    ("down", 512, 256, False),
+    ("down", 768, 256, False),
 )
 ANYWHERE = pl.BlockSpec(memory_space=pl.ANY)
 INSIDE = pl.BlockSpec(memory_space=pltpu.VMEM)
@@ -326,8 +327,8 @@
     vectors, bias_up = take(2)
     ins = dict(zip(GATHER_NAMES[1:], take(k - 1)))
     outs = dict(zip(GATHER_NAMES, take(k)))
-    tall, wsel, qkv, lse, ctx = take(5)
-    small_v, pack, vt, ct, ch, cr = take(6)
+    tall_t, wsel, qkv, lse, ctx = take(5)
+    tall, small_v, pack, vt, ct, ch, cr = take(7)
     p, s = Place(), Copies(*refs)
     me = p.xh * 4 + p.z
     peers = sp_peers(p)
@@ -429,6 +430,14 @@
         ch[t] = ct[:, t * 128 : (t + 1) * 128].T.astype(BF)
     ctx_cps = [go(ch.at[t], cr.at[me], d) for d, t in peers]
     cr[me] = ch[me]
+
+    def turn(t, _):
+        tall_t[:, pl.ds(pl.multiple_of(t * 128, 128), 128)] = tall[t].astype(F32).T.astype(BF)
+        return 0
+
+    for t in range(4):
+        lax.fori_loop(2 * t, 2 * t + 2, turn, 0)
+        advance(queue, 2)
     advance(queue, len(queue))
     for cp in ctx_cps:
         cp.wait_recv()
@@ -448,7 +457,7 @@
         shapes.append(jax.ShapeDtypeStruct((2, 4, 2) + ins[-1].shape, BF))
     k = len(shapes)
     shapes += [
-        jax.ShapeDtypeStruct((8, 128, 1024), BF),
+        jax.ShapeDtypeStruct((1024, 1024), BF),
         jax.ShapeDtypeStruct((2, 4, 2, 64, 384), BF),
         jax.ShapeDtypeStruct((1024, 384), BF),
         jax.ShapeDtypeStruct((8, 1024), F32),
@@ -460,6 +469,7 @@
         in_specs=[ANYWHERE] * 2 + [INSIDE] * 2 + [ANYWHERE] * (k - 1),
         out_specs=[ANYWHERE] * k + [INSIDE] * 5,
         scratch_shapes=[
+            pltpu.VMEM((8, 128, 1024), BF),
             pltpu.VMEM((2, 4, 2, 1, 16, 256), F32),
             pltpu.VMEM((1, 16, 256), F32),
             pltpu.VMEM((128, 1024), BF),
@@ -513,21 +523,15 @@
         self.left, self.right, self.bl, self.br = left, right, both_left, both_right
         self.sent, self.cps, self.own = [], [], []
 
-    def lanes(self, ref, at, n):
-        return ref.at[(slice(None),) * (len(ref.shape) - 1) + (pl.ds(at, n),)]
-
     def sources(self, t):
         if self.axis == "y":
             return self.left.at[:, t], self.right
         return self.left, self.right.at[:, pl.ds(pl.multiple_of(t * 1024, 128), 1024)]
 
-    def place(self):
+    def send(self, side, steps=(1, 3, 2, 0)):
         me = self.p.y if self.axis == "y" else self.p.z
-        return me, pl.multiple_of(me * 128, 128)
-
-    def send(self, side, steps=(1, 3, 2, 0)):
-        me, slot = self.place()
-        dst = self.lanes(self.bl, slot, 128) if side == 0 else self.br.at[pl.ds(slot, 128)]
+        slot = pl.multiple_of(me * 128, 128)
+        dst = self.bl.at[me] if side == 0 else self.br.at[pl.ds(slot, 128)]
         for k in steps:
             src = self.sources(lax.rem(me + k, 4))[side]
             if k == 0:
@@ -537,18 +541,16 @@
             self.cps.append(cp)
             self.sent.append(cp)
 
-    def rows_of(self, ref, c):
-        return ref.at[:, c] if self.axis == "y" else ref.at[:, :, c]
-
     def swap(self):
         p, s = self.p, self.s
         for cp in self.own:
             cp.wait()
         for cp in self.cps:
             cp.wait_recv()
-        far = self.rows_of(self.bl, 1 - p.c)
+        lead = (slice(None),) * (1 if self.axis == "y" else 2)
+        near, far = [self.bl.at[(pl.ds(k, 4),) + lead + (1 - p.c,)] for k in (0, 4)]
         self.cores = [
-            s.remote(self.lanes(far, 0, 512), self.lanes(far, 512, 512), p.to(dc=1)),
+            s.remote(near, far, p.to(dc=1)),
             s.remote(self.br.at[pl.ds(0, 512)], self.br.at[pl.ds(512, 512)], p.to(dc=1)),
         ]
         self.sent += self.cores
@@ -561,8 +563,9 @@
         n = g.shape[-1]
 
         def body(b, _):
-            left = self.bl[b, self.p.c] if self.axis == "y" else self.bl[b, :, self.p.c]
-            v = nn(left.reshape(4 * g.shape[2], 1024), self.br[:, lo : lo + n])
+            at = (b, self.p.c) if self.axis == "y" else (b, slice(None), self.p.c)
+            left = [self.bl[(k,) + at].reshape(4 * g.shape[2], 128) for k in range(8)]
+            v = nn(jnp.concatenate(left, axis=1), self.br[:, lo : lo + n])
             g[b] = v.astype(BF).reshape(4, g.shape[2], n)
             return 0
 
@@ -749,6 +752,7 @@
         bufs.append(take(3))
     do, kt, dqt, dkv, dqkv, gq, gq_c, gq_x, gq_y = take(9)
     dts, dtx, dtxr, dtz, dtz_s, dtzr = take(6)
+    bq, bq_c, bq_s, bq_x, bq_y, bw = take(6)
     vec_cp = pltpu.make_async_copy(small_h, small_v, sem.at[0])
     out_cp = pltpu.make_async_copy(out_h, w_out, sem.at[1])
     vec_cp.start()
@@ -812,6 +816,8 @@
         go(gctx.at[:, pl.ds(pl.multiple_of(t * 128, 128), 128)], do.at[me], d) for d, t in peers
     ]
     do_own = s.local(gctx.at[:, pl.ds(pl.multiple_of(me * 128, 128), 128)], do.at[me])
+    small_swap = s.remote(small_src, small_in, p.to(dc=1))
+    small_red = Reduce(p, s, "xyz", small_g, small_bufs, small_total)
     toks["down"].swap()
     red = [
         ReduceTwo(p, s, o, gi, b, totals[m].at[:, :, pl.ds(lo, n)])
@@ -831,6 +837,9 @@
 
     begin(0)
     begin(1)
+    small_swap.wait_recv()
+    small_g[...] = small_src[...] + small_in[...]
+    small_red.first()
     do_own.wait()
     for cp in do_cps:
         cp.wait_recv()
@@ -859,8 +868,10 @@
             toks["out"].swap()
         if b == 1:
             begin(3)
+            red[0].second()
         if b == 2:
             begin(4)
+            red[1].second()
     dqkv[:, :128] = dqt[...].T.astype(BF)
     dqkv[:, 128:] = dkv[...].astype(BF)
 
@@ -885,11 +896,13 @@
     lax.fori_loop(0, 4, rows_of, 0)
     c_cp = go(gq.at[:, 1 - p.c], gq_c, p.to(dc=1))
     cols = jnp.sum(dqkv[...].astype(F32), axis=0, keepdims=True)
-    small_src[me // 4, me % 4, 0, 0:1, 0:128] = cols[:, :128]
-    small_src[me // 4, me % 4, 0, 1:2, 0:128] = cols[:, 256:]
-    small_swap = s.remote(small_src, small_in, p.to(dc=1))
-    small_red = Reduce(p, s, "xyz", small_g, small_bufs, small_total)
-
+    bq[...] = jnp.zeros_like(bq)
+    bq[0:1, :] = cols[:, :128]
+    bq[1:2, :] = cols[:, 256:]
+    bc_cp = go(bq, bq_c, p.to(dc=1))
+    small_red.second()
+    red[2].second()
+    red[3].second()
     c_cp.wait_recv()
 
     def add_core(i, _):
@@ -898,9 +911,24 @@
 
     lax.fori_loop(0, 8, add_core, 0)
     x_cp = go(gq_c.at[pl.ds((1 - p.xl) * 4, 4)], gq_x, p.to(dx=1 - 2 * p.xl))
-    small_swap.wait_recv()
-    small_g[...] = small_src[...] + small_in[...]
-    small_red.first()
+    bc_cp.wait_recv()
+    bq_s[0] = bq[...] + bq_c[...]
+    bx_cp = go(bq_s.at[0], bq_x, p.to(dx=1 - 2 * p.xl))
+    red[4].second()
+    small_red.third()
+    red[0].share()
+    red[1].share()
+    x_cp.wait_recv()
+
+    def add_x(i, _):
+        gq_x[i] = (gq_x[i].astype(F32) + gq_c[p.xl * 4 + i].astype(F32)).astype(BF)
+        return 0
+
+    lax.fori_loop(0, 4, add_x, 0)
+    y_cps = [go(gq_x.at[lax.rem(p.y + d, 4)], gq_y.at[d - 1], p.to(dy=d)) for d in (1, 3, 2)]
+    bx_cp.wait_recv()
+    bq_s[1] = bq_s[0] + bq_x[...]
+    by_cps = [go(bq_s.at[1], bq_y.at[d - 1], p.to(dy=d)) for d in (1, 3, 2)]
     dx_cp.wait_recv()
 
     def add_far(i, _):
@@ -921,32 +949,26 @@
 
     lax.fori_loop(0, 2, add_round, 0)
     dx2_cp = go(dtz_s.at[1 - p.xh], dtzr, p.to(dx=2))
-    x_cp.wait_recv()
-
-    def add_x(i, _):
-        gq_x[i] = (gq_x[i].astype(F32) + gq_c[p.xl * 4 + i].astype(F32)).astype(BF)
-        return 0
-
-    lax.fori_loop(0, 4, add_x, 0)
-    y_cps = [go(gq_x.at[lax.rem(p.y + d, 4)], gq_y.at[d - 1], p.to(dy=d)) for d in (1, 3, 2)]
-    for i in range(2):
-        red[i].second()
-    small_red.second()
-    for i in range(2, len(PIECES)):
-        red[i].second()
+    red[2].share()
+    red[3].share()
+    red[4].share()
+    small_red.share()
+    red[0].spread()
+    red[1].spread()
     for cp in y_cps:
         cp.wait_recv()
     acc = gq_x[p.y].astype(F32)
     for i in range(3):
         acc = acc + gq_y[i].astype(F32)
     gw[me] = acc.astype(BF)
+    for cp in by_cps:
+        cp.wait_recv()
+    bw[me] = ((bq_s[1] + bq_y[0]) + (bq_y[1] + bq_y[2]))[0:8, :]
     gw_cps = [go(gw.at[me], gw.at[me], d) for d, _ in peers]
-    small_red.third()
-    for r in red:
-        r.share()
-    small_red.share()
-    for r in red:
-        r.spread()
+    gw_cps += [go(bw.at[me], bw.at[me], d) for d, _ in peers]
+    red[2].spread()
+    red[3].spread()
+    red[4].spread()
     small_red.spread()
     for cp in dz2_cps:
         cp.wait_recv()
@@ -968,6 +990,7 @@
         toks[m].finish()
     small_red.finish()
     small_swap.wait_send()
+    small_total[0, 0:2, 0:128] = bw[p.xl * 4 + p.y, 0:2, :]
     for cp in sent:
         cp.wait_send()
 
@@ -992,7 +1015,7 @@
     scratch += [pltpu.VMEM((2, 4, 2, ROWS[m], 128), BF) for m in GRAD_NAMES]
     scratch += [pltpu.VMEM((128, COLS[m]), BF) for m in GRAD_NAMES]
     scratch += [
-        pltpu.VMEM((2, 2, ROWS[m], 1024) if GRAD_AXIS[m] == "y" else (2, 4, 2, ROWS[m], 1024), BF)
+        pltpu.VMEM((8, 2, 2, ROWS[m], 128) if GRAD_AXIS[m] == "y" else (8, 2, 4, 2, ROWS[m], 128), BF)
         for m in GRAD_NAMES
     ]
     scratch += [pltpu.VMEM((1024, 1024), BF) for m in GRAD_NAMES]
@@ -1017,6 +1040,12 @@
         pltpu.VMEM((3, 2, 128, 512), BF),
         pltpu.VMEM((2, 128, 512), BF),
         pltpu.VMEM((128, 512), BF),
+        pltpu.VMEM((8, 128), F32),
+        pltpu.VMEM((8, 128), F32),
+        pltpu.VMEM((2, 8, 128), F32),
+        pltpu.VMEM((8, 128), F32),
+        pltpu.VMEM((3, 8, 128), F32),
+        pltpu.VMEM((8, 8, 128), F32),
     ]
     scratch += [pltpu.SemaphoreType.DMA((250,)), pltpu.SemaphoreType.DMA((250,))]
     k = len(GRAD_NAMES)
@@ -1078,7 +1107,7 @@
         shift_two=shift_two,
     )
     vectors = jnp.stack([own[k] for k in VECTORS]).astype(F32)
-    small, full_out, full_up, full_down, tall, wsel, qkv, lse, context_tokens = attend_forward(
+    small, full_out, full_up, full_down, tall_t, wsel, qkv, lse, context_tokens = attend_forward(
         inputs, w_qkv, vectors, bias_up.astype(F32).reshape(1, 256), [w_out, w_up, w_down]
     )
     grads, total, grad_inputs, output = finish_layer(
@@ -1089,7 +1118,7 @@
         full_out,
         full_up,
         full_down,
-        tall.reshape(1024, model_width).T,
+        tall_t,
         wsel,
         qkv,
         lse,

time: 209 us -> 202 us (0.967)
  Pallas kernels: 191 us -> 186 us
  local copies, waits for them, and re-layouts: 12.7 us -> 8.82 us
    pallas_call x1, Pallas kernels: 111 us -> 107 us  [finish_layer(): pl.pallas_call(backward_kernel, out_shape=[jax.ShapeDtypeStruct((4, PIECE...]
    reshape x1 -> x0, local copies, waits for them, and re-layouts: 3.93 us -> none  [on_device(): tall.reshape(1024, model_width)]
where the time goes in v2:
time: 202 us
  Pallas kernels  186 us (92%)
  local copies, waits for them, and re-layouts  8.82 us (4%)
  other arithmetic  5.7 us (3%)
    pallas_call x1, Pallas kernels, finish_layer(): pl.pallas_call(backward_kernel, out_shape=[jax.ShapeDtypeStruct((4, PIECE...  107 us
    pallas_call x1, Pallas kernels, attend_forward(): pl.pallas_call(forward_kernel, out_shape=shapes, in_specs=[ANYWHERE] * 2...  79.1 us

profile of v2, /device:TPU:0, one launch (start us, length us, event | category | flops | bytes accessed | tf_op | source)
XLA Modules:
  0.0 201.7 jit_solution(5619604486249130483)
XLA Ops:
  0.6 0.8 stack.35
  1.4 0.6 convert_element_type.37.refs_2_
  2.0 1.2 reshape.96
  3.3 79.1 %attend_forward.1 = (f32[2,4,2,1,16,256]{5,4,3,2,1,0:T(8,128)}, bf16[2,4,2,4,16,1024]{5,4,3,2,1,0:T(8,128)(2,1)}, bf16[2,4,2,4,16,4096]{5,4,3,2,1,0:T(8,128)(2,1...) custom-call(bf16[128,1024]{1,0:T(8,128)(2,1)} %bitcast.57, ...), custom_call_target="tpu_custom_call" | custom-call | tf_op jit(solution)/shard_map/attend_forward/pallas_call | solution.py:466
  82.4 107.4 %layer_back.1 = (bf16[4,64,1024]{2,1,0:T(8,128)(2,1)}, bf16[4,64,1024]{2,1,0:T(8,128)(2,1)}, bf16[4,16,1024]{2,1,0:T(8,128)(2,1)}, f32[4,8,256]{2,1,0:T(8,128)},...) custom-call(bf16[128,1024]{1,0:T(8,128)(2,1)} %bitcast.58, ...), custom_call_target="tpu_custom_call" | custom-call | tf_op jit(solution)/shard_map/layer_back/pallas_call | solution.py:1052
  189.7 0.0 copy-start
  189.8 0.0 copy-start.2
  189.8 0.0 copy-start.1
  189.8 1.5 reshape.102
  191.3 0.5 copy.32
  191.7 1.0 copy.37
  192.7 0.8 constant_dynamic-slice_fusion.1
  193.5 0.5 slice_bitcast_fusion
  194.0 1.6 bitcast_convert_fusion.1
  195.7 1.1 convert_bitcast_fusion
  196.8 1.1 copy.34
  197.9 1.3 constant_dynamic-slice_fusion
  199.2 0.0 copy-done
  199.2 1.1 bitcast_convert_fusion
  200.3 0.0 copy-done.2
  200.3 0.7 copy.40
  201.0 0.0 copy-done.1
  201.0 0.7 copy.41
Async XLA Ops:
  189.7 9.4 %copy-start = (bf16[4,64,1024]{2,1,0:T(8,128)(2,1)S(1)}, bf16[4,64,1024]{2,1,0:T(8,128)(2,1)}, u32[]{:S(2)}) copy-start(bf16[4,64,1024]{2,1,0:T(8,128)(2,1)} %get-tuple-element.46) | copy-start | bytes 1572868
  189.8 10.5 %copy-start.2 = (bf16[128,1024]{1,0:T(8,128)(2,1)S(1)}, bf16[128,1024]{1,0:T(8,128)(2,1)}, u32[]{:S(2)}) copy-start(bf16[128,1024]{1,0:T(8,128)(2,1)} %get-tuple-element.40) | copy-start | bytes 786436
  189.8 11.2 %copy-start.1 = (bf16[128,1024]{1,0:T(8,128)(2,1)S(1)}, bf16[128,1024]{1,0:T(8,128)(2,1)}, u32[]{:S(2)}) copy-start(bf16[128,1024]{1,0:T(8,128)(2,1)} %get-tuple-element.41) | copy-start | bytes 786436

commit v3 on v2

--- a/solution.py
+++ b/solution.py
@@ -719,10 +719,10 @@
 PIECE_ROWS = {"down": 64, "up": 64, "out": 16}
 PIECES = (
     ("down", 0, 512, "xz"),
-    ("down", 512, 512, "zx"),
+    ("down", 512, 512, "xz"),
     ("up", 0, 512, "yx"),
     ("up", 512, 512, "xy"),
-    ("out", 0, 1024, "zx"),
+    ("out", 0, 1024, "xz"),
 )
 
 

time: 202 us -> 208 us (1.030); the launches traced: 202 us -> 205 us
  Pallas kernels: 186 us -> 190 us
    pallas_call x1, Pallas kernels: 107 us -> 111 us  [finish_layer(): pl.pallas_call(backward_kernel, out_shape=[jax.ShapeDtypeStruct((4, PIECE...]
where the time goes in v3:
time: 208 us; the launch traced here: 205 us
  Pallas kernels  190 us (91%)
  local copies, waits for them, and re-layouts  8.82 us (4%)
  other arithmetic  5.7 us (3%)
    pallas_call x1, Pallas kernels, finish_layer(): pl.pallas_call(backward_kernel, out_shape=[jax.ShapeDtypeStruct((4, PIECE...  111 us
    pallas_call x1, Pallas kernels, attend_forward(): pl.pallas_call(forward_kernel, out_shape=shapes, in_specs=[ANYWHERE] * 2...  79.1 us

profile of v3, /device:TPU:0, one launch (start us, length us, event | category | flops | bytes accessed | tf_op | source)
XLA Modules:
  0.0 205.1 jit_solution(17832593935141739226)
XLA Ops:
  0.6 0.8 stack.35
  1.4 0.6 convert_element_type.37.refs_2_
  2.0 1.2 reshape.96
  3.3 79.1 %attend_forward.1 = (f32[2,4,2,1,16,256]{5,4,3,2,1,0:T(8,128)}, bf16[2,4,2,4,16,1024]{5,4,3,2,1,0:T(8,128)(2,1)}, bf16[2,4,2,4,16,4096]{5,4,3,2,1,0:T(8,128)(2,1...) custom-call(bf16[128,1024]{1,0:T(8,128)(2,1)} %bitcast.57, ...), custom_call_target="tpu_custom_call" | custom-call | tf_op jit(solution)/shard_map/attend_forward/pallas_call | solution.py:466
  82.4 110.7 %layer_back.1 = (bf16[4,64,1024]{2,1,0:T(8,128)(2,1)}, bf16[4,64,1024]{2,1,0:T(8,128)(2,1)}, bf16[4,16,1024]{2,1,0:T(8,128)(2,1)}, f32[4,8,256]{2,1,0:T(8,128)},...) custom-call(bf16[128,1024]{1,0:T(8,128)(2,1)} %bitcast.58, ...), custom_call_target="tpu_custom_call" | custom-call | tf_op jit(solution)/shard_map/layer_back/pallas_call | solution.py:1052
  193.1 0.0 copy-start
  193.1 0.0 copy-start.2
  193.1 0.0 copy-start.1
  193.1 1.5 reshape.102
  194.6 0.5 copy.32
  195.1 1.0 copy.37
  196.1 0.8 constant_dynamic-slice_fusion.1
  196.9 0.5 slice_bitcast_fusion
  197.4 1.6 bitcast_convert_fusion.1
  199.0 1.1 convert_bitcast_fusion
  200.2 1.1 copy.34
  201.3 1.3 constant_dynamic-slice_fusion
  202.5 0.0 copy-done
  202.5 1.1 bitcast_convert_fusion
  203.7 0.0 copy-done.2
  203.7 0.7 copy.40
  204.4 0.0 copy-done.1
  204.4 0.7 copy.41
Async XLA Ops:
  193.1 9.4 %copy-start = (bf16[4,64,1024]{2,1,0:T(8,128)(2,1)S(1)}, bf16[4,64,1024]{2,1,0:T(8,128)(2,1)}, u32[]{:S(2)}) copy-start(bf16[4,64,1024]{2,1,0:T(8,128)(2,1)} %get-tuple-element.46) | copy-start | bytes 1572868
  193.1 10.5 %copy-start.2 = (bf16[128,1024]{1,0:T(8,128)(2,1)S(1)}, bf16[128,1024]{1,0:T(8,128)(2,1)}, u32[]{:S(2)}) copy-start(bf16[128,1024]{1,0:T(8,128)(2,1)} %get-tuple-element.40) | copy-start | bytes 786436
  193.1 11.2 %copy-start.1 = (bf16[128,1024]{1,0:T(8,128)(2,1)S(1)}, bf16[128,1024]{1,0:T(8,128)(2,1)}, u32[]{:S(2)}) copy-start(bf16[128,1024]{1,0:T(8,128)(2,1)} %get-tuple-element.41) | copy-start | bytes 786436
